TPU v7x, 128 devices: a whole 4x4x4 slice. The times are simulated.
128 devices in a mesh: section: 16 (over x_hi, y, core), dp: 8 (over z, x_lo).
Axes of the slice: x: 4 (x_hi: 2, x_lo: 2; x = x_hi * 2 + x_lo), y: 4, z: 4, core: 2. Of those that a mesh axis runs over, the one named last changes fastest.
Arguments:
- tokens: bfloat16 [32768, 4096], P(('section', 'dp')), may hold values from -6 to 6
- norm_gain: float32 [4096], replicated, may hold values from 0.1 to 1.9
- gate_weight: bfloat16 [4096, 8192], P(None, 'section'), may hold values from -0.09375 to 0.09375
- up_weight: bfloat16 [4096, 8192], P(None, 'section'), may hold values from -0.09375 to 0.09375
- down_weight: bfloat16 [8192, 4096], P('section'), may hold values from -0.1875 to 0.1875
- cotangent: bfloat16 [32768, 4096], P(('section', 'dp')), may hold values from -24 to 24
Outputs:
- layer_out: bfloat16 [32768, 4096], P(('section', 'dp'))
- input_grad: bfloat16 [32768, 4096], P(('section', 'dp'))
- gate_grad: float32 [4096, 8192], P('dp', 'section')
- up_grad: float32 [4096, 8192], P('dp', 'section')
- down_grad: float32 [8192, 4096], P('section', 'dp')
All inputs are finite; a program needn't handle non-finite values.
Results may differ from a plain program's by a relative error of at most 0.018.
Values may be sent and summed in bfloat16 or wider, within the bound.
A program may use at most 192 MiB of HBM per device.

v0:
```python
import math

import jax
import jax.numpy as jnp
from jax import lax
from jax.sharding import PartitionSpec as P

ROUNDS = 2


def from_behind(array, axis, by):
    peers = lax.axis_size(axis)
    return lax.ppermute(array, axis, [(i, (i + by) % peers) for i in range(peers)])


def block_terms(normed, grad_out, weight_gate, weight_up, weight_down, factor):
    gate_act = jnp.dot(normed, weight_gate, preferred_element_type=jnp.float32)
    up_act = jnp.dot(normed, weight_up, preferred_element_type=jnp.float32)
    sigmoid_gate = jax.nn.sigmoid(gate_act)
    swish_gate = gate_act * sigmoid_gate
    hidden = (swish_gate * up_act).astype(jnp.bfloat16)
    partial_out = jnp.dot(hidden, weight_down, preferred_element_type=jnp.float32)
    grad_hidden = jnp.einsum("td,fd->tf", grad_out, weight_down, preferred_element_type=jnp.float32)
    grad_gate = (
        grad_hidden * up_act * sigmoid_gate * (1.0 + gate_act * (1.0 - sigmoid_gate))
    ).astype(jnp.bfloat16)
    grad_up = (grad_hidden * swish_gate).astype(jnp.bfloat16)
    grad_normed = jnp.einsum(
        "tf,df->td", grad_gate, weight_gate, preferred_element_type=jnp.float32
    )
    grad_normed = grad_normed + jnp.einsum(
        "tf,df->td", grad_up, weight_up, preferred_element_type=jnp.float32
    )
    term_gate = (
        jnp.einsum("td,tf->df", normed, grad_gate, preferred_element_type=jnp.float32) * factor
    )
    term_up = jnp.einsum("td,tf->df", normed, grad_up, preferred_element_type=jnp.float32) * factor
    term_down = (
        jnp.einsum("td,tf->df", grad_out, hidden, preferred_element_type=jnp.float32) * factor
    )
    return (partial_out, grad_normed, (term_gate, term_up, term_down))


def add_terms(first, second):
    return (first[0] + second[0], first[1] + second[1], first[2] + second[2])


def group_sum(terms):
    return (
        lax.psum_scatter(
            terms[0].astype(jnp.bfloat16), "dp", scatter_dimension=0, tiled=True
        ).astype(jnp.float32),
        lax.psum_scatter(
            terms[1].astype(jnp.bfloat16), "dp", scatter_dimension=0, tiled=True
        ).astype(jnp.float32),
        lax.psum_scatter(
            terms[2].astype(jnp.bfloat16), "dp", scatter_dimension=0, tiled=True
        ).astype(jnp.float32),
    )


def pass_back(terms):
    return (
        from_behind(terms[0].astype(jnp.bfloat16), "section", -1).astype(jnp.float32),
        from_behind(terms[1].astype(jnp.bfloat16), "section", -1).astype(jnp.float32),
        from_behind(terms[2].astype(jnp.bfloat16), "section", -1).astype(jnp.float32),
    )


def body(tokens, norm_gain, gate_weight, up_weight, down_weight, cotangent):
    row_count = tokens.shape[0]
    factor = 1.0 / math.sqrt(ROUNDS * lax.axis_size("dp") * row_count)
    values = tokens.astype(jnp.float32)
    inverse = lax.rsqrt(jnp.mean(values * values, axis=1, keepdims=True) + 1e-05)
    normed = (values * inverse * norm_gain).astype(jnp.bfloat16)
    totals = values
    grad_sum = jnp.zeros_like(values)
    weights = (gate_weight, up_weight, down_weight)
    held_terms = []
    for offset in range(ROUNDS):
        if offset > 0:
            weights = from_behind((weights[0], weights[1], weights[2]), "section", 1)
        partial_out, grad_normed, terms = block_terms(
            normed, cotangent, weights[0], weights[1], weights[2], factor
        )
        totals = totals + partial_out
        grad_sum = grad_sum + grad_normed
        held_terms.append(terms)
    carried = held_terms[ROUNDS - 1]
    offset = 0
    carried = add_terms(held_terms[offset], pass_back(carried))
    summed = group_sum(carried)
    scaled = grad_sum * norm_gain
    mixed = jnp.mean(scaled * values, axis=1, keepdims=True)
    input_grad = cotangent.astype(jnp.float32) + inverse * scaled - values * inverse**3 * mixed
    return (
        totals.astype(jnp.bfloat16),
        input_grad.astype(jnp.bfloat16),
        summed[0],
        summed[1],
        summed[2].T,
    )


def solution(mesh):
    in_specs = (
        P(("section", "dp"), None),
        P(),
        P(None, "section"),
        P(None, "section"),
        P("section", None),
        P(("section", "dp"), None),
    )
    out_specs = (
        P(("section", "dp"), None),
        P(("section", "dp"), None),
        P("dp", "section"),
        P("dp", "section"),
        P("section", "dp"),
    )
    return jax.shard_map(body, mesh=mesh, in_specs=in_specs, out_specs=out_specs, check_vma=False)
```

profile of v0, /device:TPU:1, one launch (start us, length us, event | category | flops | bytes accessed | tf_op | source)
XLA Modules:
  0.0 578.5 jit_solution(6864042598302475232)
XLA Ops:
  7.2 2.8 collective-permute-start.2
  10.1 1.6 collective-permute-start
  11.7 2.1 fusion.5
  13.8 42.0 %collective-permute-done.2 = bf16[512,4096]{1,0:T(8,128)(2,1)S(1)} collective-permute-done((bf16[512,4096]{1,0:T(8,128)(2,1)}, bf16[512,4096]{1,0:T(8,128)(2,1)S(1)}, u32[]{:S(2)}, u32[]{:S(2)}) %collective-permute-start.2) | collective-permute-done | bytes 4194336 | tf_op jit(solution)/shard_map/ppermute | solution.py:13
  55.7 4.4 fusion.27
  60.1 40.5 %collective-permute-done.1 = bf16[4096,512]{1,0:T(8,128)(2,1)S(1)} collective-permute-done((bf16[4096,512]{1,0:T(8,128)(2,1)}, bf16[4096,512]{1,0:T(8,128)(2,1)S(1)}, u32[]{:S(2)}, u32[]{:S(2)}) %collective-permute-start.1) | collective-permute-done | bytes 4194336 | tf_op jit(solution)/shard_map/ppermute | solution.py:13
  102.6 43.0 %collective-permute-done = bf16[4096,512]{1,0:T(8,128)(2,1)S(1)} collective-permute-done((bf16[4096,512]{1,0:T(8,128)(2,1)}, bf16[4096,512]{1,0:T(8,128)(2,1)S(1)}, u32[]{:S(2)}, u32[]{:S(2)}) %collective-permute-start) | collective-permute-done | bytes 4194336 | tf_op jit(solution)/shard_map/ppermute | solution.py:13
  145.6 1.6 multiply_convert_fusion.4
  147.6 1.4 multiply_convert_fusion.2
  149.1 5.0 collective-permute-start.3
  158.2 1.4 multiply_convert_fusion.5
  159.6 38.3 %collective-permute-done.3 = bf16[4096,512]{1,0:T(8,128)(2,1)S(1)} collective-permute-done((bf16[4096,512]{1,0:T(8,128)(2,1)S(1)}, bf16[4096,512]{1,0:T(8,128)(2,1)S(1)}, u32[]{:S(2)}, u32[]{:S(2)}) %collective-permute-start.3) | collective-permute-done | bytes 4194336 | tf_op jit(solution)/shard_map/ppermute | solution.py:13
  197.9 3.6 add_convert_fusion.1
  201.6 1.4 multiply_convert_fusion.1
  203.0 2.3 collective-permute-start.4
  205.3 45.8 %collective-permute-done.4 = bf16[4096,512]{1,0:T(8,128)(2,1)S(1)} collective-permute-done((bf16[4096,512]{1,0:T(8,128)(2,1)S(1)}, bf16[4096,512]{1,0:T(8,128)(2,1)S(1)}, u32[]{:S(2)}, u32[]{:S(2)}) %collective-permute-start.4) | collective-permute-done | bytes 4194336 | tf_op jit(solution)/shard_map/ppermute | solution.py:13
  251.1 3.7 add_convert_fusion
  254.9 3.0 fusion.1
  257.9 84.7 %collective-permute-start.5 = (bf16[4096,512]{0,1:T(8,128)(2,1)S(1)}, bf16[4096,512]{0,1:T(8,128)(2,1)S(1)}, u32[]{:S(2)}, u32[]{:S(2)}) collective-permute-start(bf16[4096,512]{0,1:T(8,128)(2,1)S(1)} %fusion.1), channel_id=1, source_target_pairs={{0,120},{8,0},{16,8},{24,16},{32,24},{40,32},{48,40},{56,48},{64,5... | collective-permute-start | bytes 12582920 | tf_op jit(solution)/shard_map/ppermute | solution.py:13
  342.5 6.8 %collective-permute-done.5 = bf16[4096,512]{0,1:T(8,128)(2,1)S(1)} collective-permute-done((bf16[4096,512]{0,1:T(8,128)(2,1)S(1)}, bf16[4096,512]{0,1:T(8,128)(2,1)S(1)}, u32[]{:S(2)}, u32[]{:S(2)}) %collective-permute-start.5) | collective-permute-done | bytes 4194336 | tf_op jit(solution)/shard_map/ppermute | solution.py:13
  349.3 3.3 fusion
  352.6 3.7 fusion.26
  358.6 1.4 convolution_add_fusion.1
  360.8 1.3 fusion.28
  363.0 1.8 fusion.11
  365.2 2.7 fusion.4
  367.9 3.1 fusion.10
  371.0 2.1 convert_element_type.84
  373.2 98.5 %reduce-scatter.6.cloned.1.call-done = bf16[512,512]{1,0:T(8,128)(2,1)} async-done(((bf16[4096,512]{1,0:T(8,128)(2,1)}), bf16[512,512]{1,0:T(8,128)(2,1)}) %reduce-scatter.6.cloned.1.call-update) | async-done | bytes 524304 | tf_op jit(solution)/shard_map/reduce_scatter | solution.py:53
  471.7 2.1 convert_element_type.88
  473.8 96.0 %reduce-scatter.8.cloned.1.call-done = bf16[512,512]{0,1:T(8,128)(2,1)} async-done(((bf16[4096,512]{0,1:T(8,128)(2,1)}), bf16[512,512]{0,1:T(8,128)(2,1)}) %reduce-scatter.8.cloned.1.call-update) | async-done | bytes 524304 | tf_op jit(solution)/shard_map/reduce_scatter | solution.py:56
  569.8 2.1 convert_bitcast_fusion
  (48 shorter events, 10.9 us)
Async XLA Ops:
  7.2 363.9 %reduce-scatter.4.cloned.1.call-start = ((), (), s32[]{:S(2)}) async-start(), calls=%async_computation.3 | async-start | bytes 4718592 | tf_op jit(solution)/shard_map/reduce_scatter | solution.py:50
  7.2 48.5 %collective-permute-start.2 = (bf16[512,4096]{1,0:T(8,128)(2,1)}, bf16[512,4096]{1,0:T(8,128)(2,1)S(1)}, u32[]{:S(2)}, u32[]{:S(2)}) collective-permute-start(bf16[512,4096]{1,0:T(8,128)(2,1)} %param.10), channel_id=1, source_target_pairs={{0,8},{8,16},{16,24},{24,32},{32,40},{40,48},{48,56},{56,64},{64,7... | collective-permute-start | bytes 12582920 | tf_op jit(solution)/shard_map/ppermute | solution.py:13
  10.0 90.7 %collective-permute-start.1 = (bf16[4096,512]{1,0:T(8,128)(2,1)}, bf16[4096,512]{1,0:T(8,128)(2,1)S(1)}, u32[]{:S(2)}, u32[]{:S(2)}) collective-permute-start(bf16[4096,512]{1,0:T(8,128)(2,1)} %param.9), channel_id=1, source_target_pairs={{0,8},{8,16},{16,24},{24,32},{32,40},{40,48},{48,56},{56,64},{64,7... | collective-permute-start | bytes 12582920 | tf_op jit(solution)/shard_map/ppermute | solution.py:13
  10.1 135.6 %collective-permute-start = (bf16[4096,512]{1,0:T(8,128)(2,1)}, bf16[4096,512]{1,0:T(8,128)(2,1)S(1)}, u32[]{:S(2)}, u32[]{:S(2)}) collective-permute-start(bf16[4096,512]{1,0:T(8,128)(2,1)} %param.8), channel_id=1, source_target_pairs={{0,8},{8,16},{16,24},{24,32},{32,40},{40,48},{48,56},{56,64},{64,7... | collective-permute-start | bytes 12582920 | tf_op jit(solution)/shard_map/ppermute | solution.py:13
  13.7 86.9 %copy-start = (bf16[256,4096]{1,0:T(8,128)(2,1)S(1)}, bf16[256,4096]{1,0:T(8,128)(2,1)}, u32[]{:S(2)}) copy-start(bf16[256,4096]{1,0:T(8,128)(2,1)} %param.6) | copy-start | bytes 6291460
  13.8 86.9 %copy-start.16 = (f32[4096]{0:T(1024)S(1)}, f32[4096]{0:T(1024)}, u32[]{:S(2)}) copy-start(f32[4096]{0:T(1024)} %param.7) | copy-start | bytes 49156
  55.7 46.3 %copy-start.11 = (bf16[512,4096]{1,0:T(8,128)(2,1)}, bf16[512,4096]{1,0:T(8,128)(2,1)S(1)}, u32[]{:S(2)}) copy-start(bf16[512,4096]{1,0:T(8,128)(2,1)S(1)} %collective-permute-done.2) | copy-start | bytes 12582916
  100.7 1.9 copy-start.7
  145.6 2.0 copy-start.13
  147.6 6.4 %copy-start.6 = (bf16[4096,512]{1,0:T(8,128)(2,1)S(1)}, bf16[4096,512]{1,0:T(8,128)(2,1)}, u32[]{:S(2)}) copy-start(bf16[4096,512]{1,0:T(8,128)(2,1)} %param.8) | copy-start | bytes 12582916
  149.1 6.3 %copy-start.4 = (bf16[4096,512]{1,0:T(8,128)(2,1)S(1)}, bf16[4096,512]{1,0:T(8,128)(2,1)}, u32[]{:S(2)}) copy-start(bf16[4096,512]{1,0:T(8,128)(2,1)} %param.9) | copy-start | bytes 12582916
  149.1 48.8 %collective-permute-start.3 = (bf16[4096,512]{1,0:T(8,128)(2,1)S(1)}, bf16[4096,512]{1,0:T(8,128)(2,1)S(1)}, u32[]{:S(2)}, u32[]{:S(2)}) collective-permute-start(bf16[4096,512]{1,0:T(8,128)(2,1)S(1)} %multiply_convert_fusion.2), channel_id=1, source_target_pairs={{0,120},{8,0},{16,8},{24,16},{32,24},{40,32},{48,40},{56,48},{64,5... | collective-permute-start | bytes 12582920 | tf_op jit(solution)/shard_map/ppermute | solution.py:13
  155.3 1.6 copy-start.1
  155.4 2.8 copy-start.9
  159.6 38.3 %copy-start.15 = (bf16[256,512]{1,0:T(8,128)(2,1)}, bf16[256,512]{1,0:T(8,128)(2,1)S(1)}, u32[]{:S(2)}) copy-start(bf16[256,512]{1,0:T(8,128)(2,1)S(1)} %get-tuple-element.9) | copy-start | bytes 786436
  201.5 270.1 %reduce-scatter.6.cloned.1.call-start = ((), (), s32[]{:S(2)}) async-start(), calls=%async_computation.4 | async-start | bytes 4718592 | tf_op jit(solution)/shard_map/reduce_scatter | solution.py:53
  203.0 48.1 %collective-permute-start.4 = (bf16[4096,512]{1,0:T(8,128)(2,1)S(1)}, bf16[4096,512]{1,0:T(8,128)(2,1)S(1)}, u32[]{:S(2)}, u32[]{:S(2)}) collective-permute-start(bf16[4096,512]{1,0:T(8,128)(2,1)S(1)} %multiply_convert_fusion.1), channel_id=1, source_target_pairs={{0,120},{8,0},{16,8},{24,16},{32,24},{40,32},{48,40},{56,48},{64,5... | collective-permute-start | bytes 12582920 | tf_op jit(solution)/shard_map/ppermute | solution.py:13
  254.8 315.0 %reduce-scatter.8.cloned.1.call-start = ((), (), s32[]{:S(2)}) async-start(), calls=%async_computation.5 | async-start | bytes 4718592 | tf_op jit(solution)/shard_map/reduce_scatter | solution.py:56
  254.9 94.5 %copy-start.2 = (bf16[256,4096]{1,0:T(8,128)(2,1)S(1)}, bf16[256,4096]{1,0:T(8,128)(2,1)}, u32[]{:S(2)}) copy-start(bf16[256,4096]{1,0:T(8,128)(2,1)} %param.11) | copy-start | bytes 6291460
  257.9 91.4 %collective-permute-start.5 = (bf16[4096,512]{0,1:T(8,128)(2,1)S(1)}, bf16[4096,512]{0,1:T(8,128)(2,1)S(1)}, u32[]{:S(2)}, u32[]{:S(2)}) collective-permute-start(bf16[4096,512]{0,1:T(8,128)(2,1)S(1)} %fusion.1), channel_id=1, source_target_pairs={{0,120},{8,0},{16,8},{24,16},{32,24},{40,32},{48,40},{56,48},{64,5... | collective-permute-start | bytes 12582920 | tf_op jit(solution)/shard_map/ppermute | solution.py:13
  352.6 3.7 copy-start.10
  356.4 2.2 copy-start.5
  358.6 2.2 copy-start.8
  360.8 2.2 copy-start.14
  363.0 2.2 copy-start.12
  365.2 2.7 copy-start.3
Sparse Core Ops, SparseCore 0:
  201.6 134.6 reduce-scatter.3
  338.8 132.8 reduce-scatter.5
  474.1 95.6 reduce-scatter.7
where the time goes:
time: 579 us; the launch traced here: 578 us
  waiting for transfers between devices  411 us (71%)
  starting transfers between devices  96.5 us (17%)
  matrix products  40 us (7%)
  between operations  14 us (2%)
  other arithmetic  11.7 us (2%)
    ppermute x6, waiting for transfers between devices, from_behind(): lax.ppermute(array, axis, [(i, (i + by) % peers) for i in range(peers)])  216 us
    reduce_scatter x1, waiting for transfers between devices, group_sum(): lax.psum_scatter(terms[1].astype(jnp.bfloat16), 'dp', scatter_dimension=0...  98.5 us
    ppermute x6, starting transfers between devices, from_behind(): lax.ppermute(array, axis, [(i, (i + by) % peers) for i in range(peers)])  96.3 us
    reduce_scatter x1, waiting for transfers between devices, group_sum(): lax.psum_scatter(terms[2].astype(jnp.bfloat16), 'dp', scatter_dimension=0...  96 us
  transfers between devices with their start and end apart: 9, of which 8 were waited for; matrix products, arithmetic and copies ran while one was open for 7% of the time, Pallas kernels for 0%

commit v1 on v0

v1 whole, which is shorter than its diff:
```python
import math

import jax
import jax.numpy as jnp
from jax import lax
from jax.sharding import PartitionSpec as P

ROUNDS = 2


def from_behind(array, axis, by):
    peers = lax.axis_size(axis)
    return lax.ppermute(array, axis, [(i, (i + by) % peers) for i in range(peers)])


def acts(normed, grad_out, weight_gate, weight_up, weight_down):
    gate_act = jnp.dot(normed, weight_gate, preferred_element_type=jnp.float32)
    up_act = jnp.dot(normed, weight_up, preferred_element_type=jnp.float32)
    sigmoid_gate = jax.nn.sigmoid(gate_act)
    swish_gate = gate_act * sigmoid_gate
    hidden = (swish_gate * up_act).astype(jnp.bfloat16)
    partial_out = jnp.dot(hidden, weight_down, preferred_element_type=jnp.float32)
    grad_hidden = jnp.einsum("td,fd->tf", grad_out, weight_down, preferred_element_type=jnp.float32)
    grad_gate = (
        grad_hidden * up_act * sigmoid_gate * (1.0 + gate_act * (1.0 - sigmoid_gate))
    ).astype(jnp.bfloat16)
    grad_up = (grad_hidden * swish_gate).astype(jnp.bfloat16)
    grad_normed = jnp.einsum(
        "tf,df->td", grad_gate, weight_gate, preferred_element_type=jnp.float32
    )
    grad_normed = grad_normed + jnp.einsum(
        "tf,df->td", grad_up, weight_up, preferred_element_type=jnp.float32
    )
    return partial_out, grad_normed, hidden, grad_gate, grad_up


def group_sum(term, axis):
    return lax.psum_scatter(
        term.astype(jnp.bfloat16), "dp", scatter_dimension=axis, tiled=True
    ).astype(jnp.float32)


def normalize(tokens, norm_gain):
    values = tokens.astype(jnp.float32)
    inverse = lax.rsqrt(jnp.mean(values * values, axis=1, keepdims=True) + 1e-05)
    return values, inverse, (values * inverse * norm_gain).astype(jnp.bfloat16)


def body(tokens, norm_gain, gate_weight, up_weight, down_weight, cotangent):
    rows = tokens.shape[0]
    factor = 1.0 / math.sqrt(ROUNDS * lax.axis_size("dp") * rows)
    next_tokens, next_cotangent = from_behind((tokens, cotangent), "section", -1)
    values, inverse, normed = normalize(tokens, norm_gain)
    weights = (gate_weight, up_weight, down_weight)
    out_a, grad_a, hidden_a, gg_a, gu_a = acts(normed, cotangent, *weights)
    _, _, next_normed = normalize(next_tokens, norm_gain)
    out_b, grad_b, hidden_b, gg_b, gu_b = acts(next_normed, next_cotangent, *weights)
    back_out, back_grad = from_behind(
        (out_b.astype(jnp.bfloat16), grad_b.astype(jnp.bfloat16)), "section", 1
    )
    all_normed = jnp.concatenate([normed, next_normed])
    all_cot = jnp.concatenate([cotangent, next_cotangent])

    def outer(a, b):
        return jnp.einsum("td,tf->df", a, b, preferred_element_type=jnp.float32) * factor

    down = group_sum(outer(jnp.concatenate([hidden_a, hidden_b]), all_cot), 1)
    gate = group_sum(outer(all_normed, jnp.concatenate([gg_a, gg_b])), 0)
    up = group_sum(outer(all_normed, jnp.concatenate([gu_a, gu_b])), 0)
    totals = values + (out_a + back_out.astype(jnp.float32))
    scaled = (grad_a + back_grad.astype(jnp.float32)) * norm_gain
    mixed = jnp.mean(scaled * values, axis=1, keepdims=True)
    input_grad = cotangent.astype(jnp.float32) + inverse * scaled - values * inverse**3 * mixed
    return (totals.astype(jnp.bfloat16), input_grad.astype(jnp.bfloat16), gate, up, down)


def solution(mesh):
    in_specs = (
        P(("section", "dp"), None),
        P(),
        P(None, "section"),
        P(None, "section"),
        P("section", None),
        P(("section", "dp"), None),
    )
    out_specs = (
        P(("section", "dp"), None),
        P(("section", "dp"), None),
        P("dp", "section"),
        P("dp", "section"),
        P("section", "dp"),
    )
    return jax.shard_map(body, mesh=mesh, in_specs=in_specs, out_specs=out_specs, check_vma=False)
```

time: 579 us -> 390 us (0.67)
  waiting for transfers between devices: 411 us -> 310 us
  starting transfers between devices: 96.5 us -> 8.24 us
    ppermute x6 -> x4, waiting for transfers between devices: 216 us -> 65 us  [from_behind(): lax.ppermute(array, axis, [(i, (i + by) % peers) for i in range(peers)])]
    ppermute x6 -> x4, starting transfers between devices: 96.3 us -> 7.94 us  [from_behind(): lax.ppermute(array, axis, [(i, (i + by) % peers) for i in range(peers)])]
    reduce_scatter x3, waiting for transfers between devices: 194 us -> 245 us  [group_sum(): lax.psum_scatter(term.astype(jnp.bfloat16), 'dp', scatter_dimension=axis,...]
    dot_general x18 -> x15, matrix products: 40 us -> 42.9 us  [the longest x3 17.1 us: outer(): jnp.einsum('td,tf->df', a, b, preferred_element_type=jnp.float32) * factor]
  transfers between devices with their start and end apart: 9 -> 7, of which waited for: 8 -> 7; matrix products, arithmetic and copies ran while one was open for 7% -> 12% of each run, Pallas kernels for 0% -> 0%
where the time goes in v1:
time: 390 us; the launch traced here: 389 us
  waiting for transfers between devices  310 us (79%)
  matrix products  42.9 us (11%)
  between operations  14 us (4%)
  other arithmetic  10.6 us (3%)
  starting transfers between devices  8.24 us (2%)
  local copies, waits for them, and re-layouts  4.01 us (1%)
    reduce_scatter x3, waiting for transfers between devices, group_sum(): lax.psum_scatter(term.astype(jnp.bfloat16), 'dp', scatter_dimension=axis,...  245 us
    ppermute x4, waiting for transfers between devices, from_behind(): lax.ppermute(array, axis, [(i, (i + by) % peers) for i in range(peers)])  65 us
    dot_general x3, matrix products, outer(): jnp.einsum('td,tf->df', a, b, preferred_element_type=jnp.float32) * factor  17.1 us
    ppermute x4, starting transfers between devices, from_behind(): lax.ppermute(array, axis, [(i, (i + by) % peers) for i in range(peers)])  7.94 us
  transfers between devices with their start and end apart: 7, of which 7 were waited for; matrix products, arithmetic and copies ran while one was open for 12% of the time, Pallas kernels for 0%

profile of v1, /device:TPU:1, one launch (start us, length us, event | category | flops | bytes accessed | tf_op | source)
XLA Modules:
  0.0 389.4 jit_solution(3696506355075378824)
XLA Ops:
  7.2 1.5 collective-permute-start
  8.7 5.0 %collective-permute-start.2 = (bf16[256,4096]{1,0:T(8,128)(2,1)}, bf16[256,4096]{1,0:T(8,128)(2,1)S(1)}, u32[]{:S(2)}, u32[]{:S(2)}) collective-permute-start(bf16[256,4096]{1,0:T(8,128)(2,1)} %param.11), channel_id=1, source_target_pairs={{0,120},{8,0},{16,8},{24,16},{32,24},{40,32},{48,40},{56,48},{64,5... | collective-permute-start | bytes 6291464 | tf_op jit(solution)/shard_map/ppermute | solution.py:13
  13.7 2.1 fusion.4
  15.8 4.2 %fusion.32 = f32[256,512]{1,0:T(8,128)S(1)} fusion(bf16[256,4096]{1,0:T(8,128)(2,1)} %param.11, bf16[512,4096]{1,0:T(8,128)(2,1)} %param.10), kind=kOutput, calls=%fused_computation.59 | convolution fusion | flops 1073741824 | bytes 6815744 | tf_op jit(solution)/shard_map/td,fd->tf/dot_general | solution.py:23
  20.1 13.8 %collective-permute-done = bf16[256,4096]{1,0:T(8,128)(2,1)S(1)} collective-permute-done((bf16[256,4096]{1,0:T(8,128)(2,1)}, bf16[256,4096]{1,0:T(8,128)(2,1)S(1)}, u32[]{:S(2)}, u32[]{:S(2)}) %collective-permute-start) | collective-permute-done | bytes 2097184 | tf_op jit(solution)/shard_map/ppermute | solution.py:13
  34.4 1.6 fusion.3
  36.6 1.2 fusion.31
  37.9 2.1 copy-done.1
  39.9 1.3 fusion.30
  41.2 1.2 fusion.29
  42.5 1.5 multiply_convert_fusion.5
  44.0 12.3 %collective-permute-done.2 = bf16[256,4096]{1,0:T(8,128)(2,1)S(1)} collective-permute-done((bf16[256,4096]{1,0:T(8,128)(2,1)}, bf16[256,4096]{1,0:T(8,128)(2,1)S(1)}, u32[]{:S(2)}, u32[]{:S(2)}) %collective-permute-start.2) | collective-permute-done | bytes 2097184 | tf_op jit(solution)/shard_map/ppermute | solution.py:13
  56.4 1.4 multiply_convert_fusion.3
  57.8 0.7 copy-done.12
  58.5 3.9 %multiply_convert_fusion = bf16[512,4096]{1,0:T(8,128)(2,1)} fusion(bf16[256,4096]{1,0:T(8,128)(2,1)S(1)} %collective-permute-done.2, bf16[256,4096]{1,0:T(8,128)(2,1)S(1)} %copy-done.7, bf16[256,512]{1,0:T(8,128)(2,1)S(1)} %get-tuple-element.9, bf16[256,512]{1,0:T(8,128)(2,1)S(1)} %get-tuple-element.12), kind=kOutput, calls=%fused_computation | convolution fusion | flops 2161115136 | bytes 8912896 | tf_op jit(solution)/shard_map/td,tf->df/dot_general | solution.py:65
  62.7 6.6 %multiply_convert_fusion.1 = bf16[4096,512]{1,0:T(8,128)(2,1)} fusion(bf16[256,4096]{1,0:T(8,128)(2,1)} %copy-done.9, bf16[256,4096]{1,0:T(8,128)(2,1)} %copy-done.10, bf16[256,512]{1,0:T(8,128)(2,1)S(1)} %get-tuple-element.7, bf16[256,512]{1,0:T(8,128)(2,1)S(1)} %get-tuple-element.10), kind=kOutput, calls=%fused_computation.1 | convolution fusion | flops 2161115136 | bytes 8912896 | tf_op jit(solution)/shard_map/td,tf->df/dot_general | solution.py:65
  69.3 6.6 %multiply_convert_fusion.2 = bf16[4096,512]{1,0:T(8,128)(2,1)} fusion(bf16[256,4096]{1,0:T(8,128)(2,1)} %copy-done.9, bf16[256,4096]{1,0:T(8,128)(2,1)} %copy-done.10, bf16[256,512]{1,0:T(8,128)(2,1)S(1)} %get-tuple-element.8, bf16[256,512]{1,0:T(8,128)(2,1)S(1)} %get-tuple-element.11), kind=kOutput, calls=%fused_computation.2 | convolution fusion | flops 2161115136 | bytes 8912896 | tf_op jit(solution)/shard_map/td,tf->df/dot_general | solution.py:65
  75.9 3.9 %fusion.34 = f32[256,4096]{1,0:T(8,128)S(1)} fusion(bf16[256,512]{1,0:T(8,128)(2,1)S(1)} %get-tuple-element.8, bf16[4096,512]{1,0:T(8,128)(2,1)} %param.8), kind=kOutput, calls=%fused_computation.61 | convolution fusion | flops 1073741824 | bytes 8650752 | tf_op jit(solution)/shard_map/tf,df->td/dot_general | solution.py:28
  79.9 1.4 fusion
  82.1 1.3 convolution_convert_fusion
  83.4 1.4 collective-permute-start.1
  84.8 1.3 fusion.33
  86.1 18.3 %collective-permute-done.3 = bf16[256,4096]{1,0:T(8,128)(2,1)S(1)} collective-permute-done((bf16[256,4096]{1,0:T(8,128)(2,1)S(1)}, bf16[256,4096]{1,0:T(8,128)(2,1)S(1)}, u32[]{:S(2)}, u32[]{:S(2)}) %collective-permute-start.3) | collective-permute-done | bytes 2097184 | tf_op jit(solution)/shard_map/ppermute | solution.py:13
  104.4 1.9 fusion.11
  106.3 20.6 %collective-permute-done.1 = bf16[256,4096]{1,0:T(8,128)(2,1)S(1)} collective-permute-done((bf16[256,4096]{1,0:T(8,128)(2,1)S(1)}, bf16[256,4096]{1,0:T(8,128)(2,1)S(1)}, u32[]{:S(2)}, u32[]{:S(2)}) %collective-permute-start.1) | collective-permute-done | bytes 2097184 | tf_op jit(solution)/shard_map/ppermute | solution.py:13
  126.9 5.0 %fusion.10 = (bf16[256,4096]{1,0:T(8,128)(2,1)}, bf16[256,4096]{1,0:T(8,128)(2,1)}) fusion(bf16[256,4096]{1,0:T(8,128)(2,1)S(1)} %copy-done, bf16[256,4096]{1,0:T(8,128)(2,1)S(1)} %copy-done.8, f32[256,4096]{1,0:T(8,128)S(1)} %get-tuple-element.18, bf16[256,4096]{1,0:T(8,128)(2,1)S(1)} %collective-permute-done.3, f32[256]{0:T(256)S(1)} %broadcast_multiply_fusion, ...), kind=kOutput, calls=%fused_computation.23 | convolution fusion | flops 1089470464 | bytes 21253120 | tf_op jit(solution)/shard_map/dot_general | solution.py:22
  131.9 27.2 %reduce-scatter.8.cloned.1.call-done = bf16[512,512]{1,0:T(8,128)(2,1)} async-done(((bf16[512,4096]{1,0:T(8,128)(2,1)}), bf16[512,512]{1,0:T(8,128)(2,1)}) %reduce-scatter.8.cloned.1.call-update) | async-done | bytes 524304 | tf_op jit(solution)/shard_map/reduce_scatter | solution.py:38
  159.1 2.1 convert_element_type.91
  161.2 125.8 %reduce-scatter.6.cloned.1.call-done = bf16[512,512]{1,0:T(8,128)(2,1)} async-done(((bf16[4096,512]{1,0:T(8,128)(2,1)}), bf16[512,512]{1,0:T(8,128)(2,1)}) %reduce-scatter.6.cloned.1.call-update) | async-done | bytes 524304 | tf_op jit(solution)/shard_map/reduce_scatter | solution.py:38
  287.0 2.1 convert_element_type.89
  289.2 91.5 %reduce-scatter.4.cloned.1.call-done = bf16[512,512]{1,0:T(8,128)(2,1)} async-done(((bf16[4096,512]{1,0:T(8,128)(2,1)}), bf16[512,512]{1,0:T(8,128)(2,1)}) %reduce-scatter.4.cloned.1.call-update) | async-done | bytes 524304 | tf_op jit(solution)/shard_map/reduce_scatter | solution.py:38
  380.7 2.1 convert_element_type.87
  (37 shorter events, 2.2 us)
Async XLA Ops:
  7.2 151.9 %reduce-scatter.8.cloned.1.call-start = ((), (), s32[]{:S(2)}) async-start(), calls=%async_computation.5 | async-start | bytes 4718592 | tf_op jit(solution)/shard_map/reduce_scatter | solution.py:38
  7.2 26.7 %collective-permute-start = (bf16[256,4096]{1,0:T(8,128)(2,1)}, bf16[256,4096]{1,0:T(8,128)(2,1)S(1)}, u32[]{:S(2)}, u32[]{:S(2)}) collective-permute-start(bf16[256,4096]{1,0:T(8,128)(2,1)} %param.6), channel_id=1, source_target_pairs={{0,120},{8,0},{16,8},{24,16},{32,24},{40,32},{48,40},{56,48},{64,5... | collective-permute-start | bytes 6291464 | tf_op jit(solution)/shard_map/ppermute | solution.py:13
  8.7 47.7 %collective-permute-start.2 = (bf16[256,4096]{1,0:T(8,128)(2,1)}, bf16[256,4096]{1,0:T(8,128)(2,1)S(1)}, u32[]{:S(2)}, u32[]{:S(2)}) collective-permute-start(bf16[256,4096]{1,0:T(8,128)(2,1)} %param.11), channel_id=1, source_target_pairs={{0,120},{8,0},{16,8},{24,16},{32,24},{40,32},{48,40},{56,48},{64,5... | collective-permute-start | bytes 6291464 | tf_op jit(solution)/shard_map/ppermute | solution.py:13
  15.8 18.6 %copy-start = (bf16[256,4096]{1,0:T(8,128)(2,1)S(1)}, bf16[256,4096]{1,0:T(8,128)(2,1)}, u32[]{:S(2)}) copy-start(bf16[256,4096]{1,0:T(8,128)(2,1)} %param.6) | copy-start | bytes 6291460
  15.8 18.6 %copy-start.11 = (f32[4096]{0:T(1024)S(1)}, f32[4096]{0:T(1024)}, u32[]{:S(2)}) copy-start(f32[4096]{0:T(1024)} %param.7) | copy-start | bytes 49156
  34.4 2.2 copy-start.3
  36.0 5.2 %copy-start.9 = (bf16[256,4096]{1,0:T(8,128)(2,1)}, bf16[256,4096]{1,0:T(8,128)(2,1)S(1)}, u32[]{:S(2)}) copy-start(bf16[256,4096]{1,0:T(8,128)(2,1)S(1)} %get-tuple-element.13) | copy-start | bytes 6291460
  36.1 6.4 %copy-start.10 = (bf16[256,4096]{1,0:T(8,128)(2,1)}, bf16[256,4096]{1,0:T(8,128)(2,1)S(1)}, u32[]{:S(2)}) copy-start(bf16[256,4096]{1,0:T(8,128)(2,1)S(1)} %get-tuple-element.14) | copy-start | bytes 6291460
  36.1 3.8 copy-start.1
  42.5 13.9 %copy-start.5 = (bf16[512,4096]{1,0:T(8,128)(2,1)S(1)}, bf16[512,4096]{1,0:T(8,128)(2,1)}, u32[]{:S(2)}) copy-start(bf16[512,4096]{1,0:T(8,128)(2,1)} %param.10) | copy-start | bytes 12582916
  44.0 14.5 %copy-start.7 = (bf16[256,4096]{1,0:T(8,128)(2,1)S(1)}, bf16[256,4096]{1,0:T(8,128)(2,1)}, u32[]{:S(2)}) copy-start(bf16[256,4096]{1,0:T(8,128)(2,1)} %param.11) | copy-start | bytes 6291460
  57.8 0.7 copy-start.12
  62.5 224.6 %reduce-scatter.6.cloned.1.call-start = ((), (), s32[]{:S(2)}) async-start(), calls=%async_computation.4 | async-start | bytes 4718592 | tf_op jit(solution)/shard_map/reduce_scatter | solution.py:38
  69.3 311.4 %reduce-scatter.4.cloned.1.call-start = ((), (), s32[]{:S(2)}) async-start(), calls=%async_computation.3 | async-start | bytes 4718592 | tf_op jit(solution)/shard_map/reduce_scatter | solution.py:38
  75.9 3.9 %copy-start.4 = (bf16[4096,512]{1,0:T(8,128)(2,1)S(1)}, bf16[4096,512]{1,0:T(8,128)(2,1)}, u32[]{:S(2)}) copy-start(bf16[4096,512]{1,0:T(8,128)(2,1)} %param.9) | copy-start | bytes 12582916
  79.9 2.2 copy-start.6
  79.9 2.2 copy-start.13
  81.3 3.5 copy-start.2
  81.3 23.1 %collective-permute-start.3 = (bf16[256,4096]{1,0:T(8,128)(2,1)S(1)}, bf16[256,4096]{1,0:T(8,128)(2,1)S(1)}, u32[]{:S(2)}, u32[]{:S(2)}) collective-permute-start(bf16[256,4096]{1,0:T(8,128)(2,1)S(1)} %fusion), channel_id=1, source_target_pairs={{0,8},{8,16},{16,24},{24,32},{32,40},{40,48},{48,56},{56,64},{64,7... | collective-permute-start | bytes 6291464 | tf_op jit(solution)/shard_map/ppermute | solution.py:13
  83.4 43.5 %collective-permute-start.1 = (bf16[256,4096]{1,0:T(8,128)(2,1)S(1)}, bf16[256,4096]{1,0:T(8,128)(2,1)S(1)}, u32[]{:S(2)}, u32[]{:S(2)}) collective-permute-start(bf16[256,4096]{1,0:T(8,128)(2,1)S(1)} %convolution_convert_fusion), channel_id=1, source_target_pairs={{0,8},{8,16},{16,24},{24,32},{32,40},{40,48},{48,56},{56,64},{64,7... | collective-permute-start | bytes 6291464 | tf_op jit(solution)/shard_map/ppermute | solution.py:13
  86.1 40.8 %copy-start.8 = (bf16[256,4096]{1,0:T(8,128)(2,1)S(1)}, bf16[256,4096]{1,0:T(8,128)(2,1)}, u32[]{:S(2)}) copy-start(bf16[256,4096]{1,0:T(8,128)(2,1)} %param.11) | copy-start | bytes 6291460
Sparse Core Ops, SparseCore 0:
  62.6 96.4 reduce-scatter.7
  161.5 125.5 reduce-scatter.5
  289.5 91.2 reduce-scatter.3

commit v2 on v1

v2 whole, which is shorter than its diff:
```python
import functools
import math

import jax
import jax.numpy as jnp
from jax import lax
from jax.experimental import pallas as pl
from jax.experimental.pallas import tpu as pltpu
from jax.sharding import PartitionSpec as P

ROUNDS = 2
GATE, UP, DOWN = 0, 1, 2
MESH = pl.DeviceIdType.MESH
F32 = jnp.float32
BF16 = jnp.bfloat16


def dot_nt(a, b):
    return lax.dot_general(a, b, (((1,), (1,)), ((), ())), preferred_element_type=F32)


def kernel(
    sections,
    tokens,
    gain_hbm,
    gate_hbm,
    up_hbm,
    down_hbm,
    cotangent,
    layer_out,
    input_grad,
    gate_grad,
    up_grad,
    down_grad,
    gain,
    weight_in,
    weight_down,
    tok,
    normed,
    cot,
    inverse,
    gate_act,
    up_act,
    acts,
    acts_t,
    scaled,
    back_out,
    back_grad,
    ret_out,
    ret_grad,
    a1_out,
    a1_in,
    a2_out,
    a2_in,
    ax_in,
    bx_out,
    bx_in,
    bz1_in,
    bz2_in,
    result,
    load_sem,
    store_sem,
    tok_sem,
    back_sem,
    a1_sem,
    a2_sem,
    ax_sem,
    bx_sem,
    bz1_sem,
    bz2_sem,
):
    rows, depth = tok.shape
    ff = weight_down.shape[0]
    half = ff // 2
    piece = depth // 8
    factor = 1.0 / math.sqrt(ROUNDS * 8 * rows)

    s = lax.axis_index("section")
    j = lax.axis_index("dp")
    core = lax.rem(s, 2)
    z, xl = j // 2, lax.rem(j, 2)
    mirrored = j + 1 - 2 * xl
    before, after = lax.rem(s + sections - 1, sections), lax.rem(s + 1, sections)
    j_before = jnp.where(lax.rem(s, 8) == 0, mirrored, j)
    j_after = jnp.where(lax.rem(after, 8) == 0, mirrored, j)
    to_before, to_after = (before, j_before), (after, j_after)
    partner = (s, mirrored)

    def plane(by):
        return lax.rem(z + by, 4)

    def neighbour(way):
        return (s, plane(1 + 2 * way) * 2 + xl)

    def remote(src, dst, sems, device):
        return pltpu.make_async_remote_copy(
            src_ref=src,
            dst_ref=dst,
            send_sem=sems.at[0],
            recv_sem=sems.at[1],
            device_id=device,
            device_id_type=MESH,
        )

    loads = [
        pltpu.make_async_copy(src, dst, load_sem.at[i])
        for i, (src, dst) in enumerate(
            (
                (tokens, tok),
                (gain_hbm, gain),
                (gate_hbm, weight_in.at[GATE]),
                (up_hbm, weight_in.at[UP]),
                (cotangent, cot.at[pl.ds(0, rows)]),
                (down_hbm, weight_down),
            )
        )
    ]
    for load in loads:
        load.start()

    barrier = pltpu.get_barrier_semaphore()
    for device in (to_before, to_after, partner, neighbour(0), neighbour(1)):
        pl.semaphore_signal(barrier, inc=1, device_id=device, device_id_type=MESH)
    pl.semaphore_wait(barrier, 5)

    send_tok = remote(tokens, normed.at[pl.ds(rows, rows)], tok_sem.at[0], to_before)
    send_cot = remote(cotangent, cot.at[pl.ds(rows, rows)], tok_sem.at[1], to_before)
    send_out = remote(back_out, ret_out, back_sem.at[0], to_after)
    send_grad = remote(back_grad, ret_grad, back_sem.at[1], to_after)
    send_tok.start()
    send_cot.start()

    def normalize(src, first, keep):
        def step(i, _):
            at = pl.ds(pl.multiple_of(i * 16, 16), 16)
            to = pl.ds(pl.multiple_of(first + i * 16, 16), 16)
            values = (src[at] if keep else src[to]).astype(F32)
            inv = lax.rsqrt(jnp.sum(values * values, axis=1, keepdims=True) / depth + 1e-05)
            if keep:
                inverse[at] = jnp.broadcast_to(inv, (16, 128))
            normed[to] = (values * inv * gain[...]).astype(BF16)
            return 0

        lax.fori_loop(0, rows // 16, step, 0)

    def forward(first):
        here = pl.ds(first, rows)

        def step(h, _):
            cols = pl.ds(pl.multiple_of(h * half, half), half)
            g = jnp.dot(normed[here], weight_in[GATE, :, cols], preferred_element_type=F32)
            u = jnp.dot(normed[here], weight_in[UP, :, cols], preferred_element_type=F32)
            gate_act[:, cols] = g
            up_act[:, cols] = u
            hidden = g * jax.nn.sigmoid(g) * u
            acts[DOWN, here, cols] = hidden.astype(BF16)
            acts_t[DOWN, cols, here] = hidden.T.astype(BF16)
            return 0

        lax.fori_loop(0, 2, step, 0)

    def backward(first):
        here = pl.ds(first, rows)

        def step(h, _):
            cols = pl.ds(pl.multiple_of(h * half, half), half)
            grad_hidden = dot_nt(cot[here], weight_down[cols])
            g, u = gate_act[:, cols], up_act[:, cols]
            sig = jax.nn.sigmoid(g)
            grad_gate = grad_hidden * u * sig * (1.0 + g * (1.0 - sig))
            grad_up = grad_hidden * (g * sig)
            acts[GATE, here, cols] = grad_gate.astype(BF16)
            acts[UP, here, cols] = grad_up.astype(BF16)
            acts_t[GATE, cols, here] = grad_gate.T.astype(BF16)
            acts_t[UP, cols, here] = grad_up.T.astype(BF16)
            return 0

        lax.fori_loop(0, 2, step, 0)

    def chunk(c):
        return pl.ds(pl.multiple_of(c * piece, piece), piece)

    def out_chunk(first, c):
        return jnp.dot(
            acts[DOWN, pl.ds(first, rows)], weight_down[:, chunk(c)], preferred_element_type=F32
        )

    def grad_chunk(first, c):
        here = pl.ds(first, rows)
        return dot_nt(acts[GATE, here], weight_in[GATE, chunk(c)]) + dot_nt(
            acts[UP, here], weight_in[UP, chunk(c)]
        )

    def return_out():
        def step(c, _):
            back_out[:, chunk(c)] = out_chunk(rows, c).astype(BF16)
            return 0

        lax.fori_loop(0, 8, step, 0)
        send_out.start()

    def return_grad():
        def step(c, _):
            back_grad[:, chunk(c)] = grad_chunk(rows, c).astype(BF16)
            return 0

        lax.fori_loop(0, 8, step, 0)
        send_grad.start()

    store_out = pltpu.make_async_copy(ret_out, layer_out, store_sem.at[0])
    store_grad = pltpu.make_async_copy(ret_grad, input_grad, store_sem.at[1])

    def finish_rows():
        send_out.wait_recv()

        def out_step(c, _):
            at = chunk(c)
            total = tok[:, at].astype(F32) + out_chunk(0, c) + ret_out[:, at].astype(F32)
            ret_out[:, at] = total.astype(BF16)
            return 0

        lax.fori_loop(0, 8, out_step, 0)
        store_out.start()
        send_grad.wait_recv()

        def grad_step(c, mixed):
            at = chunk(c)
            g = (grad_chunk(0, c) + ret_grad[:, at].astype(F32)) * gain[:, at]
            scaled[:, at] = g
            return mixed + jnp.sum(g * tok[:, at].astype(F32), axis=1, keepdims=True)

        mixed = lax.fori_loop(0, 8, grad_step, jnp.zeros((rows, 1), F32))
        inv = inverse[:, :1]
        weight = inv * inv * inv * (mixed / depth)

        def last_step(c, _):
            at = chunk(c)
            total = cot[pl.ds(0, rows), at].astype(F32) + inv * scaled[:, at]
            total = total - tok[:, at].astype(F32) * weight
            ret_grad[:, at] = total.astype(BF16)
            return 0

        lax.fori_loop(0, 8, last_step, 0)
        store_grad.start()

    def tile(which, x, to_plane, to_x, out_rows, put, adds):
        first = (to_plane * 2 + to_x) * piece
        for c in range(2):
            at = pl.ds(c * (piece // 2), piece // 2)
            cols = pl.ds(pl.multiple_of(first + c * (piece // 2), piece // 2), piece // 2)
            acc = jnp.dot(acts_t[which, out_rows], x[:, cols], preferred_element_type=F32)
            for ref in adds:
                acc = acc + ref[:, at].astype(F32)
            put(at, acc)

    def into(ref):
        def put(at, acc):
            ref[:, at] = acc.astype(BF16)

        return put

    whole = pl.ds(0, ff)

    def half_rows(h):
        return pl.ds(pl.multiple_of(h * half, half), half)

    def copy_a1(m, way):
        return remote(a1_out.at[m, way], a1_in.at[m, way], a1_sem.at[m, way], neighbour(way))

    def copy_a2(m, way, merged):
        src = a1_in.at[m, way] if merged else a2_out.at[m, way]
        return remote(
            src, a2_in.at[m, way, merged], a2_sem.at[m, way, merged], neighbour(way)
        )

    def copy_ax(m):
        return remote(a2_in.at[m, 0, xl], ax_in.at[m], ax_sem.at[m], partner)

    def copy_bx(k):
        return remote(bx_out.at[k], bx_in.at[k], bx_sem.at[k], partner)

    def copy_bz1(way):
        return remote(
            bx_in.at[0, half_rows(way)], bz1_in.at[way], bz1_sem.at[way], neighbour(way)
        )

    def copy_bz2(way, merged):
        part = way if merged else 1 - way
        return remote(
            bx_in.at[1 + way, half_rows(part)],
            bz2_in.at[way, merged],
            bz2_sem.at[way, merged],
            neighbour(way),
        )

    def a1_step(m):
        def step(way, _):
            tile(m, normed, plane(2), way, whole, into(a1_out.at[m, way]), ())
            copy_a1(m, way).start()
            return 0

        lax.fori_loop(0, 2, step, 0)

    def bx_step(k):
        by = (2, 1, 3, 0)[k]
        tile(DOWN, cot, plane(by), 1 - xl, whole, into(bx_out.at[k]), ())
        copy_bx(k).start()

    def a2_direct(m):
        def step(way, _):
            tile(m, normed, plane(1 + 2 * way), 1 - way, whole, into(a2_out.at[m, way]), ())
            copy_a2(m, way, 0).start()
            return 0

        lax.fori_loop(0, 2, step, 0)

    def a2_merged(m):
        def step(way, _):
            copy_a1(m, way).wait_recv()
            here = a1_in.at[m, way]
            tile(m, normed, plane(1 + 2 * way), way, whole, into(here), (here,))
            copy_a2(m, way, 1).start()
            return 0

        lax.fori_loop(0, 2, step, 0)

    def b_opposite():
        copy_bx(0).wait_recv()
        here = bx_in.at[0]
        tile(DOWN, cot, plane(2), xl, whole, into(here), (here,))
        copy_bz1(0).start()
        copy_bz1(1).start()

    def b_direct():
        def step(way, _):
            copy_bx(1 + way).wait_recv()
            part = half_rows(1 - way)
            here = bx_in.at[1 + way, part]
            tile(DOWN, cot, plane(1 + 2 * way), xl, part, into(here), (here,))
            copy_bz2(way, 0).start()
            return 0

        lax.fori_loop(0, 2, step, 0)

    def b_merged():
        def step(way, _):
            copy_bz1(way).wait_recv()
            part = half_rows(way)
            here = bx_in.at[1 + way, part]
            tile(DOWN, cot, plane(1 + 2 * way), xl, part, into(here), (here, bz1_in.at[way]))
            copy_bz2(way, 1).start()
            return 0

        lax.fori_loop(0, 2, step, 0)

    def a_cross(m):
        for way in range(2):
            for merged in range(2):
                copy_a2(m, way, merged).wait_recv()
        here = a2_in.at[m, 0, xl]
        tile(m, normed, z, 1 - xl, whole, into(here), (here, a2_in.at[m, 1, 1 - xl]))
        copy_ax(m).start()

    def a_last(m, out, sem):
        copy_ax(m).wait_recv()

        def put(at, acc):
            result[m, at, :] = (acc * factor).T

        adds = (a2_in.at[m, 0, 1 - xl], a2_in.at[m, 1, xl], ax_in.at[m])
        tile(m, normed, z, xl, whole, put, adds)
        copy = pltpu.make_async_copy(result.at[m], out, sem)
        copy.start()
        return copy

    def b_last(out, sem):
        copy_bx(3).wait_recv()
        for way in range(2):
            for merged in range(2):
                copy_bz2(way, merged).wait_recv()

        def step(h, _):
            part = half_rows(h)

            def put(at, acc):
                result[DOWN, part, at] = acc * factor

            adds = (bx_in.at[3, part], bz2_in.at[0, 1 - h], bz2_in.at[1, h])
            tile(DOWN, cot, z, xl, part, put, adds)
            return 0

        lax.fori_loop(0, 2, step, 0)
        copy = pltpu.make_async_copy(result.at[DOWN], out, sem)
        copy.start()
        return copy

    loads[0].wait()
    loads[1].wait()
    normalize(tok, 0, True)
    loads[2].wait()
    loads[3].wait()
    forward(0)
    loads[4].wait()
    loads[5].wait()
    backward(0)

    send_tok.wait_recv()
    normalize(normed, rows, False)
    forward(rows)
    return_out()
    send_cot.wait_recv()
    backward(rows)

    a1_step(GATE)
    bx_step(0)
    a1_step(UP)
    bx_step(1)
    bx_step(2)
    bx_step(3)
    a2_direct(GATE)
    a2_direct(UP)
    return_grad()
    a2_merged(GATE)
    b_opposite()
    a2_merged(UP)

    @pl.when(core == 1)
    def _():
        finish_rows()

    b_direct()
    b_merged()
    a_cross(GATE)
    a_cross(UP)
    stores = [b_last(down_grad, store_sem.at[2])]
    stores.append(a_last(GATE, gate_grad, store_sem.at[3]))
    stores.append(a_last(UP, up_grad, store_sem.at[4]))

    @pl.when(core == 0)
    def _():
        finish_rows()

    for copy in stores:
        copy.wait()
    store_out.wait()
    store_grad.wait()
    for copy in (send_tok, send_cot, send_out, send_grad):
        copy.wait_send()

    def drain(i, _):
        m, way = i // 2, lax.rem(i, 2)
        copy_a1(m, way).wait_send()
        for merged in range(2):
            copy_a2(m, way, merged).wait_send()
        copy_bx(i).wait_send()
        return 0

    lax.fori_loop(0, 4, drain, 0)
    for i in range(2):
        copy_ax(i).wait_send()
        copy_bz1(i).wait_send()
        copy_bz2(i, 0).wait_send()
        copy_bz2(i, 1).wait_send()


def body(sections, tokens, norm_gain, gate_weight, up_weight, down_weight, cotangent):
    rows, depth = tokens.shape
    ff = down_weight.shape[0]
    half = ff // 2
    piece = depth // 8
    anywhere = pl.BlockSpec(memory_space=pl.ANY)
    dma = pltpu.SemaphoreType.DMA

    def vmem(*shape, dtype=BF16):
        return pltpu.VMEM(shape, dtype)

    flops = 2 * 18 * rows * depth * ff
    return pl.pallas_call(
        functools.partial(kernel, sections),
        out_shape=(
            jax.ShapeDtypeStruct((rows, depth), BF16),
            jax.ShapeDtypeStruct((rows, depth), BF16),
            jax.ShapeDtypeStruct((piece, ff), F32),
            jax.ShapeDtypeStruct((piece, ff), F32),
            jax.ShapeDtypeStruct((ff, piece), F32),
        ),
        in_specs=[anywhere] * 6,
        out_specs=(anywhere,) * 5,
        scratch_shapes=[
            vmem(1, depth, dtype=F32),
            vmem(2, depth, ff),
            vmem(ff, depth),
            vmem(rows, depth),
            vmem(2 * rows, depth),
            vmem(2 * rows, depth),
            vmem(rows, 128, dtype=F32),
            vmem(rows, ff, dtype=F32),
            vmem(rows, ff, dtype=F32),
            vmem(3, 2 * rows, ff),
            vmem(3, ff, 2 * rows),
            vmem(rows, depth, dtype=F32),
            vmem(rows, depth),
            vmem(rows, depth),
            vmem(rows, depth),
            vmem(rows, depth),
            vmem(2, 2, ff, piece),
            vmem(2, 2, ff, piece),
            vmem(2, 2, ff, piece),
            vmem(2, 2, 2, ff, piece),
            vmem(2, ff, piece),
            vmem(4, ff, piece),
            vmem(4, ff, piece),
            vmem(2, half, piece),
            vmem(2, 2, half, piece),
            vmem(3, ff, piece, dtype=F32),
            dma((6,)),
            dma((5,)),
            dma((2, 2)),
            dma((2, 2)),
            dma((2, 2, 2)),
            dma((2, 2, 2, 2)),
            dma((2, 2)),
            dma((4, 2)),
            dma((2, 2)),
            dma((2, 2, 2)),
        ],
        compiler_params=pltpu.CompilerParams(
            collective_id=0, has_side_effects=True, vmem_limit_bytes=63 * 2**20
        ),
        cost_estimate=pl.CostEstimate(
            flops=flops, bytes_accessed=23 * 2**20, transcendentals=4 * rows * ff
        ),
    )(tokens, norm_gain.reshape(1, depth), gate_weight, up_weight, down_weight, cotangent)


def solution(mesh):
    in_specs = (
        P(("section", "dp"), None),
        P(),
        P(None, "section"),
        P(None, "section"),
        P("section", None),
        P(("section", "dp"), None),
    )
    out_specs = (
        P(("section", "dp"), None),
        P(("section", "dp"), None),
        P("dp", "section"),
        P("dp", "section"),
        P("section", "dp"),
    )
    return jax.shard_map(
        functools.partial(body, mesh.shape["section"]),
        mesh=mesh,
        in_specs=in_specs,
        out_specs=out_specs,
        check_vma=False,
    )
```

time: 390 us -> 126 us (0.32)
  waiting for transfers between devices: 310 us -> 0 us
  Pallas kernels: 0 us -> 116 us
  matrix products: 42.9 us -> 0 us
  between operations: 14 us -> 0.65 us
  other arithmetic: 10.6 us -> 0 us
  starting transfers between devices: 8.24 us -> 0 us
  local copies, waits for them, and re-layouts: 4.01 us -> 8.78 us
    reduce_scatter x3 -> x0, waiting for transfers between devices: 245 us -> none  [group_sum(): lax.psum_scatter(term.astype(jnp.bfloat16), 'dp', scatter_dimension=axis,...]
    pallas_call x0 -> x1, Pallas kernels: none -> 116 us  [body(): pl.pallas_call(functools.partial(kernel, sections), out_shape=(jax.ShapeD...]
    ppermute x4 -> x0, waiting for transfers between devices: 65 us -> none  [from_behind(): lax.ppermute(array, axis, [(i, (i + by) % peers) for i in range(peers)])]
    dot_general x15 -> x0, matrix products: 42.9 us -> none  [the longest x3 17.1 us: outer(): jnp.einsum('td,tf->df', a, b, preferred_element_type=jnp.float32) * factor]
    convert_element_type x4 -> x0, other arithmetic: 8.04 us -> none  [the longest x3 6.43 us: group_sum(): return lax.psum_scatter(term.astype(jnp.bfloat16), 'dp', scatter_dimensio...]
    ppermute x4 -> x0, starting transfers between devices: 7.94 us -> none  [from_behind(): lax.ppermute(array, axis, [(i, (i + by) % peers) for i in range(peers)])]
    unnamed x28 -> x13, local copies, waits for them, and re-layouts: 4.01 us -> 8.78 us
  transfers between devices with their start and end apart: 7 -> 0, of which waited for: 7 -> 0; matrix products, arithmetic and copies ran while one was open for 12% -> 0% of each run, Pallas kernels for 0% -> 0%
where the time goes in v2:
time: 126 us
  Pallas kernels  116 us (92%)
  local copies, waits for them, and re-layouts  8.78 us (7%)
    pallas_call x1, Pallas kernels, body(): pl.pallas_call(functools.partial(kernel, sections), out_shape=(jax.ShapeD...  116 us
    unnamed x13, local copies, waits for them, and re-layouts  8.78 us

profile of v2, /device:TPU:1, one launch (start us, length us, event | category | flops | bytes accessed | tf_op | source)
XLA Modules:
  0.0 125.8 jit_solution(9720678737722404026)
XLA Ops:
  0.6 116.3 %shard_map.101 = (bf16[256,4096]{1,0:T(8,128)(2,1)}, bf16[256,4096]{1,0:T(8,128)(2,1)}, f32[512,512]{1,0:T(8,128)}, f32[512,512]{1,0:T(8,128)}, f32[512,512]{1,0:T(8,128)}) custom-call(bf16[256,4096]{1,0:T(8,128)(2,1)} %tokens.1, f32[1,4096]{1,0:T(1,128)} %bitcast.1, bf16[4096,512]{1,0:T(8,128)(2,1)} %gate_hbm.1, bf16[4096,512]{1,0:T(8,128)(2,1)} %up_hbm.1, ...), custom_call_target="tpu_custom_call" | custom-call | flops 19327352832 | bytes 24117248 | tf_op jit(solution)/shard_map/pallas_call | solution.py:478
  117.0 0.0 copy-start
  117.0 3.3 %copy.16 = bf16[256,4096]{1,0:T(8,128)(2,1)} copy(bf16[256,4096]{1,0:T(8,128)(2,1)} %get-tuple-element.10) | data formatting | bytes 4194304
  120.3 0.0 copy-done
  120.3 0.0 copy-start.3
  120.3 1.3 %copy.17 = bf16[256,4096]{1,0:T(8,128)(2,1)} copy(bf16[256,4096]{1,0:T(8,128)(2,1)S(1)} %copy-done) | data formatting | bytes 4194304
  121.6 0.6 copy-done.3
  122.2 0.0 copy-start.2
  122.2 0.0 copy-start.1
  122.2 1.0 copy.18
  123.2 0.6 copy-done.2
  123.8 1.0 copy.19
  124.8 0.0 copy-done.1
  124.8 1.0 copy.20
Async XLA Ops:
  117.0 3.3 %copy-start = (bf16[256,4096]{1,0:T(8,128)(2,1)S(1)}, bf16[256,4096]{1,0:T(8,128)(2,1)}, u32[]{:S(2)}) copy-start(bf16[256,4096]{1,0:T(8,128)(2,1)} %get-tuple-element.11) | copy-start | bytes 6291460
  120.3 2.0 %copy-start.3 = (f32[512,512]{1,0:T(8,128)S(1)}, f32[512,512]{1,0:T(8,128)}, u32[]{:S(2)}) copy-start(f32[512,512]{1,0:T(8,128)} %get-tuple-element.12) | copy-start | bytes 3145732
  122.2 1.6 %copy-start.2 = (f32[512,512]{1,0:T(8,128)S(1)}, f32[512,512]{1,0:T(8,128)}, u32[]{:S(2)}) copy-start(f32[512,512]{1,0:T(8,128)} %get-tuple-element.13) | copy-start | bytes 3145732
  122.2 2.6 %copy-start.1 = (f32[512,512]{1,0:T(8,128)S(1)}, f32[512,512]{1,0:T(8,128)}, u32[]{:S(2)}) copy-start(f32[512,512]{1,0:T(8,128)} %get-tuple-element.14) | copy-start | bytes 3145732

commit v3 on v2

v3 whole, which is shorter than its diff:
```python
import functools
import math

import jax
import jax.numpy as jnp
from jax import lax
from jax.experimental import pallas as pl
from jax.experimental.pallas import tpu as pltpu
from jax.sharding import PartitionSpec as P

ROUNDS = 2
GATE, UP, DOWN = 0, 1, 2
MESH = pl.DeviceIdType.MESH
F32 = jnp.float32
BF16 = jnp.bfloat16


def dot_nt(a, b):
    return lax.dot_general(a, b, (((1,), (1,)), ((), ())), preferred_element_type=F32)


def kernel(
    sections,
    tokens,
    gain_hbm,
    gate_hbm,
    up_hbm,
    down_hbm,
    cotangent,
    layer_out,
    input_grad,
    gate_grad,
    up_grad,
    down_grad,
    gain,
    weight_in,
    weight_down,
    tok,
    normed,
    cot,
    inverse,
    gate_act,
    up_act,
    acts,
    acts_t,
    scaled,
    back_out,
    back_grad,
    ret_out,
    ret_grad,
    a1_out,
    a1_in,
    a2_out,
    a2_in,
    ax_in,
    far_normed,
    far_acts,
    bo_out,
    bd_out,
    b1_in,
    b2_in,
    result,
    load_sem,
    store_sem,
    tok_sem,
    back_sem,
    a1_sem,
    a2_sem,
    ax_sem,
    near_sem,
    rest_sem,
    pass_sem,
    far_sem,
    b1_sem,
    b2_sem,
):
    rows, depth = tok.shape
    ff = weight_down.shape[0]
    half = ff // 2
    piece = depth // 8
    factor = 1.0 / math.sqrt(ROUNDS * 8 * rows)
    own, met = pl.ds(0, rows), pl.ds(rows, rows)

    s = lax.axis_index("section")
    j = lax.axis_index("dp")
    core = lax.rem(s, 2)
    z, xl = j // 2, lax.rem(j, 2)
    mirrored = j + 1 - 2 * xl
    before, after = lax.rem(s + sections - 1, sections), lax.rem(s + 1, sections)
    j_before = jnp.where(lax.rem(s, 8) == 0, mirrored, j)
    j_after = jnp.where(lax.rem(after, 8) == 0, mirrored, j)
    to_before, to_after = (before, j_before), (after, j_after)
    partner = (s, mirrored)

    def plane(by):
        return lax.rem(z + by, 4)

    def neighbour(way):
        return (s, plane(1 + 2 * way) * 2 + xl)

    def remote(src, dst, sems, device):
        return pltpu.make_async_remote_copy(
            src_ref=src,
            dst_ref=dst,
            send_sem=sems.at[0],
            recv_sem=sems.at[1],
            device_id=device,
            device_id_type=MESH,
        )

    loads = [
        pltpu.make_async_copy(src, dst, load_sem.at[i])
        for i, (src, dst) in enumerate(
            (
                (tokens, tok),
                (gain_hbm, gain),
                (gate_hbm, weight_in.at[GATE]),
                (up_hbm, weight_in.at[UP]),
                (cotangent, cot.at[pl.ds(0, rows)]),
                (down_hbm, weight_down),
            )
        )
    ]
    for load in loads:
        load.start()

    barrier = pltpu.get_barrier_semaphore()
    for device in (to_before, to_after, partner, neighbour(0), neighbour(1)):
        pl.semaphore_signal(barrier, inc=1, device_id=device, device_id_type=MESH)
    pl.semaphore_wait(barrier, 5)

    send_tok = remote(tokens, normed.at[pl.ds(rows, rows)], tok_sem.at[0], to_before)
    send_cot = remote(cotangent, cot.at[pl.ds(rows, rows)], tok_sem.at[1], to_before)
    send_out = remote(back_out, ret_out, back_sem.at[0], to_after)
    send_grad = remote(back_grad, ret_grad, back_sem.at[1], to_after)
    send_tok.start()
    send_cot.start()

    def normalize(src, first, keep):
        def step(i, _):
            at = pl.ds(pl.multiple_of(i * 16, 16), 16)
            to = pl.ds(pl.multiple_of(first + i * 16, 16), 16)
            values = (src[at] if keep else src[to]).astype(F32)
            inv = lax.rsqrt(jnp.sum(values * values, axis=1, keepdims=True) / depth + 1e-05)
            if keep:
                inverse[at] = jnp.broadcast_to(inv, (16, 128))
            normed[to] = (values * inv * gain[...]).astype(BF16)
            return 0

        lax.fori_loop(0, rows // 16, step, 0)

    def forward(first):
        here = pl.ds(first, rows)

        def step(h, _):
            cols = pl.ds(pl.multiple_of(h * half, half), half)
            g = jnp.dot(normed[here], weight_in[GATE, :, cols], preferred_element_type=F32)
            u = jnp.dot(normed[here], weight_in[UP, :, cols], preferred_element_type=F32)
            gate_act[here, cols] = g
            up_act[here, cols] = u
            hidden = g * jax.nn.sigmoid(g) * u
            acts[DOWN, here, cols] = hidden.astype(BF16)
            acts_t[DOWN, cols, here] = hidden.T.astype(BF16)
            return 0

        lax.fori_loop(0, 2, step, 0)

    def backward(first):
        here = pl.ds(first, rows)

        def step(h, _):
            cols = pl.ds(pl.multiple_of(h * half, half), half)
            grad_hidden = dot_nt(cot[here], weight_down[cols])
            g, u = gate_act[here, cols], up_act[here, cols]
            sig = jax.nn.sigmoid(g)
            grad_gate = grad_hidden * u * sig * (1.0 + g * (1.0 - sig))
            grad_up = grad_hidden * (g * sig)
            acts[GATE, here, cols] = grad_gate.astype(BF16)
            acts[UP, here, cols] = grad_up.astype(BF16)
            acts_t[GATE, cols, here] = grad_gate.T.astype(BF16)
            acts_t[UP, cols, here] = grad_up.T.astype(BF16)
            return 0

        lax.fori_loop(0, 2, step, 0)

    def chunk(c):
        return pl.ds(pl.multiple_of(c * piece, piece), piece)

    def out_chunk(first, c):
        return jnp.dot(
            acts[DOWN, pl.ds(first, rows)], weight_down[:, chunk(c)], preferred_element_type=F32
        )

    def grad_chunk(first, c):
        here = pl.ds(first, rows)
        return dot_nt(acts[GATE, here], weight_in[GATE, chunk(c)]) + dot_nt(
            acts[UP, here], weight_in[UP, chunk(c)]
        )

    def return_out():
        def step(c, _):
            back_out[:, chunk(c)] = out_chunk(rows, c).astype(BF16)
            return 0

        lax.fori_loop(0, 8, step, 0)
        send_out.start()

    def return_grad():
        def step(c, _):
            back_grad[:, chunk(c)] = grad_chunk(rows, c).astype(BF16)
            return 0

        lax.fori_loop(0, 8, step, 0)
        send_grad.start()

    store_out = pltpu.make_async_copy(ret_out, layer_out, store_sem.at[0])
    store_grad = pltpu.make_async_copy(ret_grad, input_grad, store_sem.at[1])

    def finish_out():
        send_out.wait_recv()

        def step(c, _):
            at = chunk(c)
            total = tok[:, at].astype(F32) + out_chunk(0, c) + ret_out[:, at].astype(F32)
            ret_out[:, at] = total.astype(BF16)
            return 0

        lax.fori_loop(0, 8, step, 0)
        store_out.start()

    def own_grad():
        def step(c, _):
            scaled[:, chunk(c)] = grad_chunk(0, c)
            return 0

        lax.fori_loop(0, 8, step, 0)

    def finish_grad():
        send_grad.wait_recv()

        def grad_step(c, mixed):
            at = chunk(c)
            g = (scaled[:, at] + ret_grad[:, at].astype(F32)) * gain[:, at]
            scaled[:, at] = g
            return mixed + jnp.sum(g * tok[:, at].astype(F32), axis=1, keepdims=True)

        mixed = lax.fori_loop(0, 8, grad_step, jnp.zeros((rows, 1), F32))
        inv = inverse[:, :1]
        weight = inv * inv * inv * (mixed / depth)

        def last_step(c, _):
            at = chunk(c)
            total = cot[own, at].astype(F32) + inv * scaled[:, at]
            total = total - tok[:, at].astype(F32) * weight
            ret_grad[:, at] = total.astype(BF16)
            return 0

        lax.fori_loop(0, 8, last_step, 0)
        store_grad.start()

    whole = pl.ds(0, ff)

    def half_rows(h):
        return pl.ds(pl.multiple_of(h * half, half), half)

    def into(ref):
        def put(at, acc):
            ref[:, at] = acc.astype(BF16)

        return put

    def down_tile(to_plane, to_x, put, adds):
        first = (to_plane * 2 + to_x) * piece
        for c in range(2):
            at = pl.ds(c * (piece // 2), piece // 2)
            cols = pl.ds(pl.multiple_of(first + c * (piece // 2), piece // 2), piece // 2)
            acc = jnp.dot(acts_t[DOWN], cot[:, cols], preferred_element_type=F32)
            for ref in adds:
                acc = acc + ref[:, at].astype(F32)
            put(at, acc)

    def in_tile(m, to_plane, part, put, adds):
        cols = pl.ds(pl.multiple_of((to_plane * 2 + xl) * piece, piece), piece)
        acc = jnp.dot(acts_t[m, part], normed[:, cols], preferred_element_type=F32)
        acc = acc + jnp.dot(far_acts[m, part], far_normed[to_plane], preferred_element_type=F32)
        for ref in adds:
            acc = acc + ref[...].astype(F32)
        put(pl.ds(0, piece), acc)

    def two(step):
        def run(i, _):
            step(i)
            return 0

        lax.fori_loop(0, 2, run, 0)

    def copy_a1(way):
        return remote(a1_out.at[way], a1_in.at[way], a1_sem.at[way], neighbour(way))

    def copy_a2(way, merged):
        src = a1_in.at[way] if merged else a2_out.at[way]
        return remote(src, a2_in.at[way, merged], a2_sem.at[way, merged], neighbour(way))

    copy_ax = remote(a2_in.at[0, xl], ax_in, ax_sem, partner)

    def a_opposite(way):
        down_tile(plane(2), way, into(a1_out.at[way]), ())
        copy_a1(way).start()

    def a_direct(way):
        down_tile(plane(1 + 2 * way), 1 - way, into(a2_out.at[way]), ())
        copy_a2(way, 0).start()

    def a_merged(way):
        copy_a1(way).wait_recv()
        here = a1_in.at[way]
        down_tile(plane(1 + 2 * way), way, into(here), (here,))
        copy_a2(way, 1).start()

    def a_cross():
        for way in range(2):
            for merged in range(2):
                copy_a2(way, merged).wait_recv()
        here = a2_in.at[0, xl]
        down_tile(z, 1 - xl, into(here), (here, a2_in.at[1, 1 - xl]))
        copy_ax.start()

    def store(m, out):
        copy = pltpu.make_async_copy(result.at[m], out, store_sem.at[2 + m])
        copy.start()
        return copy

    def a_last():
        copy_ax.wait_recv()

        def put(at, acc):
            result[DOWN, :, at] = (acc * factor).astype(BF16)

        down_tile(z, xl, put, (a2_in.at[0, 1 - xl], a2_in.at[1, xl], ax_in))
        return store(DOWN, down_grad)

    def far_columns(zz):
        return pl.ds(pl.multiple_of((zz * 2 + 1 - xl) * piece, piece), piece)

    def copy_near(zz):
        return remote(
            normed.at[own, far_columns(zz)], far_normed.at[zz, own], near_sem.at[zz], partner
        )

    def copy_rest(zz):
        return remote(
            normed.at[met, far_columns(zz)], far_normed.at[zz, met], rest_sem.at[zz], partner
        )

    def copy_pass(zz):
        return pltpu.make_async_remote_copy(
            src_ref=far_normed.at[zz, own],
            dst_ref=far_normed.at[zz, met],
            send_sem=pass_sem.at[zz],
            recv_sem=rest_sem.at[zz, 1],
            device_id=to_before,
            device_id_type=MESH,
        )

    def copy_far(m):
        return remote(acts_t.at[m], far_acts.at[m], far_sem.at[m], partner)

    def copy_b1(m, way):
        return remote(
            bo_out.at[m, half_rows(way)], b1_in.at[m, way], b1_sem.at[m, way], neighbour(way)
        )

    def copy_b2(m, way, merged):
        src = b1_in.at[m, way] if merged else bd_out.at[m, way]
        return remote(src, b2_in.at[m, way, merged], b2_sem.at[m, way, merged], neighbour(way))

    def b_first(m):
        copy_far(m).wait_recv()

        def opposite(way):
            part = half_rows(way)
            in_tile(m, plane(2), part, into(bo_out.at[m, part]), ())
            copy_b1(m, way).start()

        def direct(way):
            in_tile(m, plane(1 + 2 * way), half_rows(1 - way), into(bd_out.at[m, way]), ())
            copy_b2(m, way, 0).start()

        two(opposite)
        two(direct)

    def b_merged(m):
        def step(way):
            copy_b1(m, way).wait_recv()
            here = b1_in.at[m, way]
            in_tile(m, plane(1 + 2 * way), half_rows(way), into(here), (here,))
            copy_b2(m, way, 1).start()

        two(step)

    def b_last(m, out):
        for way in range(2):
            for merged in range(2):
                copy_b2(m, way, merged).wait_recv()

        def step(h):
            part = half_rows(h)

            def put(at, acc):
                result[m, part, at] = (acc * factor).astype(BF16)

            in_tile(m, z, part, put, (b2_in.at[m, 0, 1 - h], b2_in.at[m, 1, h]))

        two(step)
        return store(m, out)

    loads[0].wait()
    loads[1].wait()
    normalize(tok, 0, True)
    for zz in range(4):
        copy_near(zz).start()
    loads[2].wait()
    loads[3].wait()
    forward(0)
    loads[4].wait()
    loads[5].wait()

    @pl.when(core == 1)
    def _():
        backward(0)
        own_grad()

    send_tok.wait_recv()
    normalize(normed, rows, False)

    @pl.when(core == 1)
    def _():
        for zz in range(4):
            copy_rest(zz).start()

    forward(rows)

    @pl.when(core == 1)
    def _():
        return_out()
        for zz in range(4):
            copy_near(zz).wait_recv()
            copy_pass(zz).start()

    send_cot.wait_recv()
    two(a_opposite)
    two(a_direct)

    @pl.when(core == 0)
    def _():
        backward(0)

    backward(rows)
    copy_far(GATE).start()
    copy_far(UP).start()

    @pl.when(core == 1)
    def _():
        return_grad()

    two(a_merged)

    @pl.when(core == 0)
    def _():
        return_out()
        return_grad()
        own_grad()
        for zz in range(4):
            copy_near(zz).wait_recv()

    @pl.when(core == 1)
    def _():
        finish_out()
        finish_grad()

    for zz in range(4):
        copy_rest(zz).wait_recv()
    b_first(GATE)
    b_first(UP)
    a_cross()
    b_merged(GATE)
    b_merged(UP)
    stores = [a_last()]
    stores.append(b_last(GATE, gate_grad))
    stores.append(b_last(UP, up_grad))

    @pl.when(core == 0)
    def _():
        finish_out()
        finish_grad()

    for copy in stores:
        copy.wait()
    store_out.wait()
    store_grad.wait()
    for copy in (send_tok, send_cot, send_out, send_grad, copy_ax):
        copy.wait_send()
    for zz in range(4):
        copy_near(zz).wait_send()

    @pl.when(core == 1)
    def _():
        for zz in range(4):
            copy_rest(zz).wait_send()
            copy_pass(zz).wait_send()

    for i in range(2):
        copy_a1(i).wait_send()
        copy_far(i).wait_send()
        for k in range(2):
            copy_a2(i, k).wait_send()
            copy_b1(i, k).wait_send()
            copy_b2(i, k, 0).wait_send()
            copy_b2(i, k, 1).wait_send()


def write_out(
    layer_in,
    input_in,
    gate_in,
    up_in,
    down_in,
    layer_out,
    input_grad,
    gate_grad,
    up_grad,
    down_grad,
    near,
    far,
    sems,
):
    rows = [
        pltpu.make_async_copy(src, dst, sems.at[i])
        for i, (src, dst) in enumerate(((layer_in, layer_out), (input_in, input_grad)))
    ]
    loads = [
        pltpu.make_async_copy(src, near.at[i], sems.at[2 + i])
        for i, src in enumerate((gate_in, up_in, down_in))
    ]
    stores = [
        pltpu.make_async_copy(far.at[i], dst, sems.at[5 + i])
        for i, dst in enumerate((gate_grad, up_grad, down_grad))
    ]
    for copy in loads + rows:
        copy.start()
    for m in (GATE, UP, DOWN):
        loads[m].wait()
        if m == DOWN:
            far[m] = near[m].astype(F32)
        else:
            far[m] = near[m].astype(F32).T
        stores[m].start()
    for copy in stores + rows:
        copy.wait()


def body(sections, tokens, norm_gain, gate_weight, up_weight, down_weight, cotangent):
    rows, depth = tokens.shape
    ff = down_weight.shape[0]
    half = ff // 2
    piece = depth // 8
    anywhere = pl.BlockSpec(memory_space=pl.ANY)
    dma = pltpu.SemaphoreType.DMA

    def vmem(*shape, dtype=BF16):
        return pltpu.VMEM(shape, dtype)

    flops = 2 * 18 * rows * depth * ff
    parts = pl.pallas_call(
        functools.partial(kernel, sections),
        out_shape=(
            jax.ShapeDtypeStruct((rows, depth), BF16),
            jax.ShapeDtypeStruct((rows, depth), BF16),
            jax.ShapeDtypeStruct((ff, piece), BF16),
            jax.ShapeDtypeStruct((ff, piece), BF16),
            jax.ShapeDtypeStruct((ff, piece), BF16),
        ),
        in_specs=[anywhere] * 6,
        out_specs=(anywhere,) * 5,
        scratch_shapes=[
            vmem(1, depth, dtype=F32),
            vmem(2, depth, ff),
            vmem(ff, depth),
            vmem(rows, depth),
            vmem(2 * rows, depth),
            vmem(2 * rows, depth),
            vmem(rows, 128, dtype=F32),
            vmem(2 * rows, ff, dtype=F32),
            vmem(2 * rows, ff, dtype=F32),
            vmem(3, 2 * rows, ff),
            vmem(3, ff, 2 * rows),
            vmem(rows, depth, dtype=F32),
            vmem(rows, depth),
            vmem(rows, depth),
            vmem(rows, depth),
            vmem(rows, depth),
            vmem(2, ff, piece),
            vmem(2, ff, piece),
            vmem(2, ff, piece),
            vmem(2, 2, ff, piece),
            vmem(ff, piece),
            vmem(4, 2 * rows, piece),
            vmem(2, ff, 2 * rows),
            vmem(2, ff, piece),
            vmem(2, 2, half, piece),
            vmem(2, 2, half, piece),
            vmem(2, 2, 2, half, piece),
            vmem(3, ff, piece),
            dma((6,)),
            dma((5,)),
            dma((2, 2)),
            dma((2, 2)),
            dma((2, 2)),
            dma((2, 2, 2)),
            dma((2,)),
            dma((4, 2)),
            dma((4, 2)),
            dma((4,)),
            dma((2, 2)),
            dma((2, 2, 2)),
            dma((2, 2, 2, 2)),
        ],
        compiler_params=pltpu.CompilerParams(
            collective_id=0, has_side_effects=True, vmem_limit_bytes=63 * 2**20
        ),
        cost_estimate=pl.CostEstimate(
            flops=flops, bytes_accessed=23 * 2**20, transcendentals=4 * rows * ff
        ),
    )(tokens, norm_gain.reshape(1, depth), gate_weight, up_weight, down_weight, cotangent)
    return pl.pallas_call(
        write_out,
        out_shape=(
            jax.ShapeDtypeStruct((rows, depth), BF16),
            jax.ShapeDtypeStruct((rows, depth), BF16),
            jax.ShapeDtypeStruct((piece, ff), F32),
            jax.ShapeDtypeStruct((piece, ff), F32),
            jax.ShapeDtypeStruct((ff, piece), F32),
        ),
        in_specs=[anywhere] * 5,
        out_specs=(anywhere,) * 5,
        scratch_shapes=[vmem(3, ff, piece), vmem(3, ff, piece, dtype=F32), dma((8,))],
        compiler_params=pltpu.CompilerParams(vmem_limit_bytes=32 * 2**20),
        cost_estimate=pl.CostEstimate(flops=0, bytes_accessed=13 * 2**20, transcendentals=0),
    )(*parts)


def solution(mesh):
    in_specs = (
        P(("section", "dp"), None),
        P(),
        P(None, "section"),
        P(None, "section"),
        P("section", None),
        P(("section", "dp"), None),
    )
    out_specs = (
        P(("section", "dp"), None),
        P(("section", "dp"), None),
        P("dp", "section"),
        P("dp", "section"),
        P("section", "dp"),
    )
    return jax.shard_map(
        functools.partial(body, mesh.shape["section"]),
        mesh=mesh,
        in_specs=in_specs,
        out_specs=out_specs,
        check_vma=False,
    )
```

time: 126 us -> 114 us (0.905)
  Pallas kernels: 116 us -> 106 us
  local copies, waits for them, and re-layouts: 8.78 us -> 6.3 us
    pallas_call x1, Pallas kernels: 116 us -> 103 us  [body(): pl.pallas_call(functools.partial(kernel, sections), out_shape=(jax.ShapeD...]
    pallas_call x0 -> x1, Pallas kernels: none -> 3.16 us  [body(): pl.pallas_call(write_out, out_shape=(jax.ShapeDtypeStruct((rows, depth),...]
    unnamed x13 -> x10, local copies, waits for them, and re-layouts: 8.78 us -> 6.3 us
where the time goes in v3:
time: 114 us; the launch traced here: 113 us
  Pallas kernels  106 us (93%)
  local copies, waits for them, and re-layouts  6.3 us (6%)
    pallas_call x1, Pallas kernels, body(): pl.pallas_call(functools.partial(kernel, sections), out_shape=(jax.ShapeD...  103 us
    unnamed x10, local copies, waits for them, and re-layouts  6.3 us
    pallas_call x1, Pallas kernels, body(): pl.pallas_call(write_out, out_shape=(jax.ShapeDtypeStruct((rows, depth),...  3.16 us

profile of v3, /device:TPU:1, one launch (start us, length us, event | category | flops | bytes accessed | tf_op | source)
XLA Modules:
  0.0 113.4 jit_solution(13521505447418498718)
XLA Ops:
  0.6 103.3 %shard_map.101 = (bf16[256,4096]{1,0:T(8,128)(2,1)}, bf16[256,4096]{1,0:T(8,128)(2,1)}, bf16[512,512]{1,0:T(8,128)(2,1)}, bf16[512,512]{1,0:T(8,128)(2,1)}, bf16[512,512]{1,0:T(8,128)(2,1)}) custom-call(bf16[256,4096]{1,0:T(8,128)(2,1)} %tokens.1, f32[1,4096]{1,0:T(1,128)} %bitcast.1, bf16[4096,512]{1,0:T(8,128)(2,1)} %gate_hbm.1, bf16[4096,512]{1,0:T(8,128)(2,1)} %up_hbm.1, ...), custom_call_target="tpu_custom_call" | custom-call | flops 19327352832 | bytes 24117248 | tf_op jit(solution)/shard_map/pallas_call | solution.py:574
  104.0 0.0 copy-start
  104.0 1.6 %copy-done = bf16[256,4096]{1,0:T(8,128)(2,1)S(1)} copy-done((bf16[256,4096]{1,0:T(8,128)(2,1)S(1)}, bf16[256,4096]{1,0:T(8,128)(2,1)}, u32[]{:S(2)}) %copy-start) | copy-done | bytes 2097176
  105.5 0.0 copy-start.1
  105.5 1.6 %copy-done.1 = bf16[256,4096]{1,0:T(8,128)(2,1)S(1)} copy-done((bf16[256,4096]{1,0:T(8,128)(2,1)S(1)}, bf16[256,4096]{1,0:T(8,128)(2,1)}, u32[]{:S(2)}) %copy-start.1) | copy-done | bytes 2097176
  107.1 0.0 copy-start.2
  107.1 1.0 copy-done.2
  108.2 0.0 copy-start.3
  108.2 1.0 copy-done.3
  109.2 0.0 copy-start.4
  109.2 1.0 copy-done.4
  110.3 3.2 %shard_map.102 = (bf16[256,4096]{1,0:T(8,128)(2,1)}, bf16[256,4096]{1,0:T(8,128)(2,1)}, f32[512,512]{1,0:T(8,128)}, f32[512,512]{1,0:T(8,128)}, f32[512,512]{1,0:T(8,128)}) custom-call(bf16[256,4096]{1,0:T(8,128)(2,1)S(1)} %copy-done, bf16[256,4096]{1,0:T(8,128)(2,1)S(1)} %copy-done.1, bf16[512,512]{1,0:T(8,128)(2,1)S(1)} %copy-done.2, ...), custom_call_target="tpu_custom_call" | custom-call | bytes 13631488 | tf_op jit(solution)/shard_map/pallas_call | solution.py:635
Async XLA Ops:
  104.0 1.6 %copy-start = (bf16[256,4096]{1,0:T(8,128)(2,1)S(1)}, bf16[256,4096]{1,0:T(8,128)(2,1)}, u32[]{:S(2)}) copy-start(bf16[256,4096]{1,0:T(8,128)(2,1)} %get-tuple-element.10.layer_in) | copy-start | bytes 6291460
  105.5 1.6 %copy-start.1 = (bf16[256,4096]{1,0:T(8,128)(2,1)S(1)}, bf16[256,4096]{1,0:T(8,128)(2,1)}, u32[]{:S(2)}) copy-start(bf16[256,4096]{1,0:T(8,128)(2,1)} %get-tuple-element.11.input_in) | copy-start | bytes 6291460
  107.1 1.0 copy-start.2
  108.2 1.0 copy-start.3
  109.2 1.0 copy-start.4

commit v4 on v3

--- a/solution.py
+++ b/solution.py
@@ -57,6 +57,7 @@
     far_acts,
     bo_out,
     bd_out,
+    held,
     b1_in,
     b2_in,
     result,
@@ -129,14 +130,41 @@
         pl.semaphore_signal(barrier, inc=1, device_id=device, device_id_type=MESH)
     pl.semaphore_wait(barrier, 5)
 
-    send_tok = remote(tokens, normed.at[pl.ds(rows, rows)], tok_sem.at[0], to_before)
-    send_cot = remote(cotangent, cot.at[pl.ds(rows, rows)], tok_sem.at[1], to_before)
-    send_out = remote(back_out, ret_out, back_sem.at[0], to_after)
-    send_grad = remote(back_grad, ret_grad, back_sem.at[1], to_after)
-    send_tok.start()
-    send_cot.start()
-
-    def normalize(src, first, keep):
+    part = rows // 2
+    send_tok = [
+        remote(
+            tokens.at[pl.ds(i * part, part)],
+            normed.at[pl.ds(rows + i * part, part)],
+            tok_sem.at[2 + i],
+            to_before,
+        )
+        for i in range(2)
+    ]
+    send_cot = [
+        remote(
+            cotangent.at[pl.ds(i * part, part)],
+            cot.at[pl.ds(rows + i * part, part)],
+            tok_sem.at[i],
+            to_before,
+        )
+        for i in range(2)
+    ]
+    send_out, send_grad = (
+        [
+            remote(
+                src.at[pl.ds(i * part, part)],
+                dst.at[pl.ds(i * part, part)],
+                back_sem.at[k, i],
+                to_after,
+            )
+            for i in range(2)
+        ]
+        for k, (src, dst) in enumerate(((back_out, ret_out), (back_grad, ret_grad)))
+    )
+    for copy in (*send_tok, *send_cot):
+        copy.start()
+
+    def normalize(src, first, count, keep):
         def step(i, _):
             at = pl.ds(pl.multiple_of(i * 16, 16), 16)
             to = pl.ds(pl.multiple_of(first + i * 16, 16), 16)
@@ -147,10 +175,10 @@
             normed[to] = (values * inv * gain[...]).astype(BF16)
             return 0
 
-        lax.fori_loop(0, rows // 16, step, 0)
-
-    def forward(first):
-        here = pl.ds(first, rows)
+        lax.fori_loop(0, count // 16, step, 0, unroll=2)
+
+    def forward(first, count):
+        here = pl.ds(first, count)
 
         def step(h, _):
             cols = pl.ds(pl.multiple_of(h * half, half), half)
@@ -165,8 +193,8 @@
 
         lax.fori_loop(0, 2, step, 0)
 
-    def backward(first):
-        here = pl.ds(first, rows)
+    def backward(first, count):
+        here = pl.ds(first, count)
 
         def step(h, _):
             cols = pl.ds(pl.multiple_of(h * half, half), half)
@@ -186,42 +214,55 @@
     def chunk(c):
         return pl.ds(pl.multiple_of(c * piece, piece), piece)
 
-    def out_chunk(first, c):
+    def out_chunk(first, count, c):
         return jnp.dot(
-            acts[DOWN, pl.ds(first, rows)], weight_down[:, chunk(c)], preferred_element_type=F32
-        )
-
-    def grad_chunk(first, c):
-        here = pl.ds(first, rows)
+            acts[DOWN, pl.ds(first, count)], weight_down[:, chunk(c)], preferred_element_type=F32
+        )
+
+    def grad_chunk(first, count, c):
+        here = pl.ds(first, count)
         return dot_nt(acts[GATE, here], weight_in[GATE, chunk(c)]) + dot_nt(
             acts[UP, here], weight_in[UP, chunk(c)]
         )
 
-    def return_out():
+    def return_out(first, count):
         def step(c, _):
-            back_out[:, chunk(c)] = out_chunk(rows, c).astype(BF16)
+            back_out[pl.ds(first, count), chunk(c)] = out_chunk(rows + first, count, c).astype(BF16)
             return 0
 
         lax.fori_loop(0, 8, step, 0)
-        send_out.start()
-
-    def return_grad():
+
+    def return_grad(i):
         def step(c, _):
-            back_grad[:, chunk(c)] = grad_chunk(rows, c).astype(BF16)
+            back_grad[pl.ds(i * part, part), chunk(c)] = grad_chunk(
+                rows + i * part, part, c
+            ).astype(BF16)
             return 0
 
         lax.fori_loop(0, 8, step, 0)
-        send_grad.start()
+        send_grad[i].start()
+
+    def both_grads():
+        def step(c, _):
+            g = grad_chunk(0, 2 * rows, c)
+            scaled[:, chunk(c)] = g[:rows]
+            back_grad[:, chunk(c)] = g[rows:].astype(BF16)
+            return 0
+
+        lax.fori_loop(0, 8, step, 0)
+        for copy in send_grad:
+            copy.start()
 
     store_out = pltpu.make_async_copy(ret_out, layer_out, store_sem.at[0])
     store_grad = pltpu.make_async_copy(ret_grad, input_grad, store_sem.at[1])
 
     def finish_out():
-        send_out.wait_recv()
+        for copy in send_out:
+            copy.wait_recv()
 
         def step(c, _):
             at = chunk(c)
-            total = tok[:, at].astype(F32) + out_chunk(0, c) + ret_out[:, at].astype(F32)
+            total = tok[:, at].astype(F32) + out_chunk(0, rows, c) + ret_out[:, at].astype(F32)
             ret_out[:, at] = total.astype(BF16)
             return 0
 
@@ -230,13 +271,14 @@
 
     def own_grad():
         def step(c, _):
-            scaled[:, chunk(c)] = grad_chunk(0, c)
+            scaled[:, chunk(c)] = grad_chunk(0, rows, c)
             return 0
 
         lax.fori_loop(0, 8, step, 0)
 
     def finish_grad():
-        send_grad.wait_recv()
+        for copy in send_grad:
+            copy.wait_recv()
 
         def grad_step(c, mixed):
             at = chunk(c)
@@ -279,13 +321,10 @@
                 acc = acc + ref[:, at].astype(F32)
             put(at, acc)
 
-    def in_tile(m, to_plane, part, put, adds):
+    def in_tile(m, to_plane):
         cols = pl.ds(pl.multiple_of((to_plane * 2 + xl) * piece, piece), piece)
-        acc = jnp.dot(acts_t[m, part], normed[:, cols], preferred_element_type=F32)
-        acc = acc + jnp.dot(far_acts[m, part], far_normed[to_plane], preferred_element_type=F32)
-        for ref in adds:
-            acc = acc + ref[...].astype(F32)
-        put(pl.ds(0, piece), acc)
+        acc = jnp.dot(acts_t[m], normed[:, cols], preferred_element_type=F32)
+        return acc + jnp.dot(far_acts[m], far_normed[to_plane], preferred_element_type=F32)
 
     def two(step):
         def run(i, _):
@@ -342,10 +381,19 @@
     def far_columns(zz):
         return pl.ds(pl.multiple_of((zz * 2 + 1 - xl) * piece, piece), piece)
 
+    need = (2, 1, 3, 0)
+
     def copy_near(zz):
         return remote(
             normed.at[own, far_columns(zz)], far_normed.at[zz, own], near_sem.at[zz], partner
         )
+
+    def start_near(k):
+        copy_near(plane(need[k])).start()
+
+    def pass_on(k):
+        copy_near(plane(need[k])).wait_recv()
+        copy_pass(plane(need[k])).start()
 
     def copy_rest(zz):
         return remote(
@@ -374,132 +422,165 @@
         src = b1_in.at[m, way] if merged else bd_out.at[m, way]
         return remote(src, b2_in.at[m, way, merged], b2_sem.at[m, way, merged], neighbour(way))
 
+    own_tile = (gate_act, up_act)
+
+    def arrived(by):
+        @pl.when(core == 0)
+        def _():
+            copy_near(plane(by)).wait_recv()
+
+        copy_rest(plane(by)).wait_recv()
+
     def b_first(m):
         copy_far(m).wait_recv()
-
-        def opposite(way):
-            part = half_rows(way)
-            in_tile(m, plane(2), part, into(bo_out.at[m, part]), ())
+        if m == GATE:
+            arrived(2)
+        bo_out[m] = in_tile(m, plane(2)).astype(BF16)
+        for way in range(2):
             copy_b1(m, way).start()
-
-        def direct(way):
-            in_tile(m, plane(1 + 2 * way), half_rows(1 - way), into(bd_out.at[m, way]), ())
+        for way in range(2):
+            if m == GATE:
+                arrived(1 + 2 * way)
+            tile = in_tile(m, plane(1 + 2 * way))
+            straight, later = (tile[half:], tile[:half]) if way == 0 else (tile[:half], tile[half:])
+            bd_out[m, way] = straight.astype(BF16)
             copy_b2(m, way, 0).start()
-
-        two(opposite)
-        two(direct)
+            held[m, way] = later
+
+    def b_own():
+        arrived(0)
+        for m in (GATE, UP):
+            own_tile[m][...] = in_tile(m, z)
 
     def b_merged(m):
-        def step(way):
+        for way in range(2):
             copy_b1(m, way).wait_recv()
-            here = b1_in.at[m, way]
-            in_tile(m, plane(1 + 2 * way), half_rows(way), into(here), (here,))
+            b1_in[m, way] = (held[m, way] + b1_in[m, way].astype(F32)).astype(BF16)
             copy_b2(m, way, 1).start()
-
-        two(step)
 
     def b_last(m, out):
         for way in range(2):
             for merged in range(2):
                 copy_b2(m, way, merged).wait_recv()
-
-        def step(h):
-            part = half_rows(h)
-
-            def put(at, acc):
-                result[m, part, at] = (acc * factor).astype(BF16)
-
-            in_tile(m, z, part, put, (b2_in.at[m, 0, 1 - h], b2_in.at[m, 1, h]))
-
-        two(step)
+        for h in range(2):
+            at = pl.ds(h * half, half)
+            total = own_tile[m][at] + b2_in[m, 0, 1 - h].astype(F32) + b2_in[m, 1, h].astype(F32)
+            result[m, at] = (total * factor).astype(BF16)
         return store(m, out)
 
     loads[0].wait()
     loads[1].wait()
-    normalize(tok, 0, True)
-    for zz in range(4):
-        copy_near(zz).start()
-    loads[2].wait()
-    loads[3].wait()
-    forward(0)
-    loads[4].wait()
-    loads[5].wait()
+    normalize(tok, 0, rows, True)
+    start_near(0)
+    start_near(1)
+
+    @pl.when(core == 0)
+    def _():
+        loads[2].wait()
+        loads[3].wait()
+        forward(0, rows)
+        for copy in send_tok:
+            copy.wait_recv()
+        normalize(normed, rows, rows, False)
+        forward(rows, rows)
+        loads[4].wait()
+        loads[5].wait()
+        for copy in send_cot:
+            copy.wait_recv()
 
     @pl.when(core == 1)
     def _():
-        backward(0)
+        loads[2].wait()
+        loads[3].wait()
+        forward(0, rows)
+        loads[4].wait()
+        loads[5].wait()
+        backward(0, rows)
         own_grad()
-
-    send_tok.wait_recv()
-    normalize(normed, rows, False)
-
-    @pl.when(core == 1)
-    def _():
-        for zz in range(4):
-            copy_rest(zz).start()
-
-    forward(rows)
-
-    @pl.when(core == 1)
-    def _():
-        return_out()
-        for zz in range(4):
-            copy_near(zz).wait_recv()
-            copy_pass(zz).start()
-
-    send_cot.wait_recv()
-    two(a_opposite)
-    two(a_direct)
-
-    @pl.when(core == 0)
-    def _():
-        backward(0)
-
-    backward(rows)
-    copy_far(GATE).start()
-    copy_far(UP).start()
-
-    @pl.when(core == 1)
-    def _():
-        return_grad()
-
-    two(a_merged)
-
-    @pl.when(core == 0)
-    def _():
-        return_out()
-        return_grad()
-        own_grad()
-        for zz in range(4):
-            copy_near(zz).wait_recv()
-
-    @pl.when(core == 1)
-    def _():
+        pass_on(0)
+        pass_on(1)
+        start_near(2)
+        for i in range(2):
+            send_tok[i].wait_recv()
+            start_near(3) if i == 0 else pass_on(2)
+            normalize(normed, rows + i * part, part, False)
+            forward(rows + i * part, part)
+            return_out(i * part, part)
+            send_out[i].start()
+        pass_on(3)
+        for by in need:
+            copy_rest(plane(by)).start()
         finish_out()
         finish_grad()
-
-    for zz in range(4):
-        copy_rest(zz).wait_recv()
+        send_cot[0].wait_recv()
+        backward(rows, part)
+        return_grad(0)
+        send_cot[1].wait_recv()
+
+    two(a_opposite)
+
+    @pl.when(core == 0)
+    def _():
+        backward(0, 2 * rows)
+
+    @pl.when(core == 1)
+    def _():
+        backward(rows + part, part)
+
+    copy_far(GATE).start()
+    two(a_direct)
+
+    @pl.when(core == 0)
+    def _():
+        start_near(2)
+
+    copy_far(UP).start()
+    two(a_merged)
+
+    @pl.when(core == 1)
+    def _():
+        return_grad(1)
+
+    @pl.when(core == 0)
+    def _():
+        start_near(3)
+        return_out(0, rows)
+        for copy in send_out:
+            copy.start()
+        both_grads()
+
     b_first(GATE)
     b_first(UP)
-    a_cross()
+
+    @pl.when(core == 1)
+    def _():
+        a_cross()
+        b_own()
+
     b_merged(GATE)
     b_merged(UP)
+
+    @pl.when(core == 0)
+    def _():
+        a_cross()
+        b_own()
+        finish_out()
+
     stores = [a_last()]
     stores.append(b_last(GATE, gate_grad))
     stores.append(b_last(UP, up_grad))
 
     @pl.when(core == 0)
     def _():
-        finish_out()
         finish_grad()
 
     for copy in stores:
         copy.wait()
     store_out.wait()
     store_grad.wait()
-    for copy in (send_tok, send_cot, send_out, send_grad, copy_ax):
+    for copy in (*send_tok, *send_cot, *send_out, *send_grad, copy_ax):
         copy.wait_send()
+
     for zz in range(4):
         copy_near(zz).wait_send()
 
@@ -530,23 +611,36 @@
     gate_grad,
     up_grad,
     down_grad,
+    rows,
     near,
     far,
     sems,
 ):
-    rows = [
-        pltpu.make_async_copy(src, dst, sems.at[i])
-        for i, (src, dst) in enumerate(((layer_in, layer_out), (input_in, input_grad)))
-    ]
     loads = [
-        pltpu.make_async_copy(src, near.at[i], sems.at[2 + i])
-        for i, src in enumerate((gate_in, up_in, down_in))
+        pltpu.make_async_copy(src, dst, sems.at[0, i])
+        for i, (src, dst) in enumerate(
+            (
+                (gate_in, near.at[GATE]),
+                (up_in, near.at[UP]),
+                (down_in, near.at[DOWN]),
+                (layer_in, rows.at[0]),
+                (input_in, rows.at[1]),
+            )
+        )
     ]
     stores = [
-        pltpu.make_async_copy(far.at[i], dst, sems.at[5 + i])
-        for i, dst in enumerate((gate_grad, up_grad, down_grad))
+        pltpu.make_async_copy(src, dst, sems.at[1, i])
+        for i, (src, dst) in enumerate(
+            (
+                (far.at[GATE], gate_grad),
+                (far.at[UP], up_grad),
+                (far.at[DOWN], down_grad),
+                (rows.at[0], layer_out),
+                (rows.at[1], input_grad),
+            )
+        )
     ]
-    for copy in loads + rows:
+    for copy in loads:
         copy.start()
     for m in (GATE, UP, DOWN):
         loads[m].wait()
@@ -555,7 +649,10 @@
         else:
             far[m] = near[m].astype(F32).T
         stores[m].start()
-    for copy in stores + rows:
+    for i in (3, 4):
+        loads[i].wait()
+        stores[i].start()
+    for copy in stores:
         copy.wait()
 
 
@@ -608,13 +705,14 @@
             vmem(2, ff, 2 * rows),
             vmem(2, ff, piece),
             vmem(2, 2, half, piece),
+            vmem(2, 2, half, piece, dtype=F32),
             vmem(2, 2, half, piece),
             vmem(2, 2, 2, half, piece),
             vmem(3, ff, piece),
             dma((6,)),
             dma((5,)),
-            dma((2, 2)),
-            dma((2, 2)),
+            dma((4, 2)),
+            dma((2, 2, 2)),
             dma((2, 2)),
             dma((2, 2, 2)),
             dma((2,)),
@@ -643,8 +741,13 @@
         ),
         in_specs=[anywhere] * 5,
         out_specs=(anywhere,) * 5,
-        scratch_shapes=[vmem(3, ff, piece), vmem(3, ff, piece, dtype=F32), dma((8,))],
-        compiler_params=pltpu.CompilerParams(vmem_limit_bytes=32 * 2**20),
+        scratch_shapes=[
+            vmem(2, rows, depth),
+            vmem(3, ff, piece),
+            vmem(3, ff, piece, dtype=F32),
+            dma((2, 5)),
+        ],
+        compiler_params=pltpu.CompilerParams(vmem_limit_bytes=63 * 2**20),
         cost_estimate=pl.CostEstimate(flops=0, bytes_accessed=13 * 2**20, transcendentals=0),
     )(*parts)
 

time: 114 us -> 101 us (0.89)
  the two profiles are of different devices: /device:TPU:1 before, /device:TPU:25 now
where the time goes in v4:
time: 101 us
  Pallas kernels  100 us (99%)
    pallas_call x1, Pallas kernels, body(): pl.pallas_call(functools.partial(kernel, sections), out_shape=(jax.ShapeD...  95.1 us
    pallas_call x1, Pallas kernels, body(): pl.pallas_call(write_out, out_shape=(jax.ShapeDtypeStruct((rows, depth),...  5.22 us

profile of v4, /device:TPU:25, one launch (start us, length us, event | category | flops | bytes accessed | tf_op | source)
XLA Modules:
  0.0 101.2 jit_solution(15533520156378231582)
XLA Ops:
  0.6 95.1 %shard_map.101 = (bf16[256,4096]{1,0:T(8,128)(2,1)}, bf16[256,4096]{1,0:T(8,128)(2,1)}, bf16[512,512]{1,0:T(8,128)(2,1)}, bf16[512,512]{1,0:T(8,128)(2,1)}, bf16[512,512]{1,0:T(8,128)(2,1)}) custom-call(bf16[256,4096]{1,0:T(8,128)(2,1)} %tokens.1, f32[1,4096]{1,0:T(1,128)} %bitcast.1, bf16[4096,512]{1,0:T(8,128)(2,1)} %gate_hbm.1, bf16[4096,512]{1,0:T(8,128)(2,1)} %up_hbm.1, ...), custom_call_target="tpu_custom_call" | custom-call | flops 19327352832 | bytes 24117248 | tf_op jit(solution)/shard_map/pallas_call | solution.py:671
  95.8 5.2 %shard_map.102 = (bf16[256,4096]{1,0:T(8,128)(2,1)}, bf16[256,4096]{1,0:T(8,128)(2,1)}, f32[512,512]{1,0:T(8,128)}, f32[512,512]{1,0:T(8,128)}, f32[512,512]{1,0:T(8,128)}) custom-call(bf16[256,4096]{1,0:T(8,128)(2,1)} %get-tuple-element.10.layer_in, bf16[256,4096]{1,0:T(8,128)(2,1)} %get-tuple-element.11.input_in, ...), custom_call_target="tpu_custom_call" | custom-call | bytes 13631488 | tf_op jit(solution)/shard_map/pallas_call | solution.py:733

commit v5 on v4

--- a/solution.py
+++ b/solution.py
@@ -41,6 +41,7 @@
     inverse,
     gate_act,
     up_act,
+    grad_hidden,
     acts,
     acts_t,
     scaled,
@@ -135,32 +136,38 @@
         remote(
             tokens.at[pl.ds(i * part, part)],
             normed.at[pl.ds(rows + i * part, part)],
-            tok_sem.at[2 + i],
+            tok_sem.at[4 + i],
             to_before,
         )
         for i in range(2)
     ]
+    need = (2, 1, 3, 0)
+
+    def slab(by):
+        return pl.ds(pl.multiple_of(plane(by) * 2 * piece, 2 * piece), 2 * piece)
+
     send_cot = [
+        remote(cotangent.at[:, slab(by)], cot.at[met, slab(by)], tok_sem.at[i], to_before)
+        for i, by in enumerate(need)
+    ]
+    send_out = [
         remote(
-            cotangent.at[pl.ds(i * part, part)],
-            cot.at[pl.ds(rows + i * part, part)],
-            tok_sem.at[i],
-            to_before,
+            back_out.at[pl.ds(i * part, part)],
+            ret_out.at[pl.ds(i * part, part)],
+            back_sem.at[i],
+            to_after,
         )
         for i in range(2)
     ]
-    send_out, send_grad = (
-        [
-            remote(
-                src.at[pl.ds(i * part, part)],
-                dst.at[pl.ds(i * part, part)],
-                back_sem.at[k, i],
-                to_after,
-            )
-            for i in range(2)
-        ]
-        for k, (src, dst) in enumerate(((back_out, ret_out), (back_grad, ret_grad)))
-    )
+    send_grad = [
+        remote(
+            back_grad.at[:, pl.ds(i * 2 * piece, 2 * piece)],
+            ret_grad.at[:, pl.ds(i * 2 * piece, 2 * piece)],
+            back_sem.at[2 + i],
+            to_after,
+        )
+        for i in range(4)
+    ]
     for copy in (*send_tok, *send_cot):
         copy.start()
 
@@ -193,20 +200,39 @@
 
         lax.fori_loop(0, 2, step, 0)
 
+    def backward_part(here, cols, grad_hidden):
+        g, u = gate_act[here, cols], up_act[here, cols]
+        sig = jax.nn.sigmoid(g)
+        grad_gate = grad_hidden * u * sig * (1.0 + g * (1.0 - sig))
+        grad_up = grad_hidden * (g * sig)
+        acts[GATE, here, cols] = grad_gate.astype(BF16)
+        acts[UP, here, cols] = grad_up.astype(BF16)
+        acts_t[GATE, cols, here] = grad_gate.T.astype(BF16)
+        acts_t[UP, cols, here] = grad_up.T.astype(BF16)
+
     def backward(first, count):
         here = pl.ds(first, count)
 
         def step(h, _):
             cols = pl.ds(pl.multiple_of(h * half, half), half)
-            grad_hidden = dot_nt(cot[here], weight_down[cols])
-            g, u = gate_act[here, cols], up_act[here, cols]
-            sig = jax.nn.sigmoid(g)
-            grad_gate = grad_hidden * u * sig * (1.0 + g * (1.0 - sig))
-            grad_up = grad_hidden * (g * sig)
-            acts[GATE, here, cols] = grad_gate.astype(BF16)
-            acts[UP, here, cols] = grad_up.astype(BF16)
-            acts_t[GATE, cols, here] = grad_gate.T.astype(BF16)
-            acts_t[UP, cols, here] = grad_up.T.astype(BF16)
+            backward_part(here, cols, dot_nt(cot[here], weight_down[cols]))
+            return 0
+
+        lax.fori_loop(0, 2, step, 0)
+
+    def met_slab(by):
+        def step(h, _):
+            cols = pl.ds(pl.multiple_of(h * half, half), half)
+            term = dot_nt(cot[met, slab(by)], weight_down[cols, slab(by)])
+            grad_hidden[:, cols] = term if by == need[0] else grad_hidden[:, cols] + term
+            return 0
+
+        lax.fori_loop(0, 2, step, 0)
+
+    def backward_met():
+        def step(h, _):
+            cols = pl.ds(pl.multiple_of(h * half, half), half)
+            backward_part(met, cols, grad_hidden[:, cols])
             return 0
 
         lax.fori_loop(0, 2, step, 0)
@@ -232,15 +258,15 @@
 
         lax.fori_loop(0, 8, step, 0)
 
-    def return_grad(i):
-        def step(c, _):
-            back_grad[pl.ds(i * part, part), chunk(c)] = grad_chunk(
-                rows + i * part, part, c
-            ).astype(BF16)
-            return 0
-
-        lax.fori_loop(0, 8, step, 0)
-        send_grad[i].start()
+    def return_grad():
+        for i in range(4):
+
+            def step(c, _):
+                back_grad[:, chunk(c)] = grad_chunk(rows, rows, c).astype(BF16)
+                return 0
+
+            lax.fori_loop(2 * i, 2 * i + 2, step, 0)
+            send_grad[i].start()
 
     def both_grads():
         def step(c, _):
@@ -380,8 +406,6 @@
 
     def far_columns(zz):
         return pl.ds(pl.multiple_of((zz * 2 + 1 - xl) * piece, piece), piece)
-
-    need = (2, 1, 3, 0)
 
     def copy_near(zz):
         return remote(
@@ -487,6 +511,18 @@
         loads[5].wait()
         for copy in send_cot:
             copy.wait_recv()
+        two(a_opposite)
+        backward(0, 2 * rows)
+        copy_far(GATE).start()
+        two(a_direct)
+        start_near(2)
+        copy_far(UP).start()
+        two(a_merged)
+        start_near(3)
+        return_out(0, rows)
+        for copy in send_out:
+            copy.start()
+        both_grads()
 
     @pl.when(core == 1)
     def _():
@@ -510,44 +546,24 @@
         pass_on(3)
         for by in need:
             copy_rest(plane(by)).start()
+        send_cot[0].wait_recv()
+        two(a_opposite)
+        met_slab(2)
         finish_out()
         finish_grad()
-        send_cot[0].wait_recv()
-        backward(rows, part)
-        return_grad(0)
         send_cot[1].wait_recv()
-
-    two(a_opposite)
-
-    @pl.when(core == 0)
-    def _():
-        backward(0, 2 * rows)
-
-    @pl.when(core == 1)
-    def _():
-        backward(rows + part, part)
-
-    copy_far(GATE).start()
-    two(a_direct)
-
-    @pl.when(core == 0)
-    def _():
-        start_near(2)
-
-    copy_far(UP).start()
-    two(a_merged)
-
-    @pl.when(core == 1)
-    def _():
-        return_grad(1)
-
-    @pl.when(core == 0)
-    def _():
-        start_near(3)
-        return_out(0, rows)
-        for copy in send_out:
-            copy.start()
-        both_grads()
+        a_direct(0)
+        met_slab(1)
+        send_cot[2].wait_recv()
+        a_direct(1)
+        met_slab(3)
+        two(a_merged)
+        send_cot[3].wait_recv()
+        met_slab(0)
+        backward_met()
+        copy_far(GATE).start()
+        copy_far(UP).start()
+        return_grad()
 
     b_first(GATE)
     b_first(UP)
@@ -640,8 +656,11 @@
             )
         )
     ]
-    for copy in loads:
-        copy.start()
+    for i in (3, 4, 0, 1, 2):
+        loads[i].start()
+    for i in (3, 4):
+        loads[i].wait()
+        stores[i].start()
     for m in (GATE, UP, DOWN):
         loads[m].wait()
         if m == DOWN:
@@ -649,9 +668,6 @@
         else:
             far[m] = near[m].astype(F32).T
         stores[m].start()
-    for i in (3, 4):
-        loads[i].wait()
-        stores[i].start()
     for copy in stores:
         copy.wait()
 
@@ -689,6 +705,7 @@
             vmem(rows, 128, dtype=F32),
             vmem(2 * rows, ff, dtype=F32),
             vmem(2 * rows, ff, dtype=F32),
+            vmem(rows, ff, dtype=F32),
             vmem(3, 2 * rows, ff),
             vmem(3, ff, 2 * rows),
             vmem(rows, depth, dtype=F32),
@@ -711,8 +728,8 @@
             vmem(3, ff, piece),
             dma((6,)),
             dma((5,)),
-            dma((4, 2)),
-            dma((2, 2, 2)),
+            dma((6, 2)),
+            dma((6, 2)),
             dma((2, 2)),
             dma((2, 2, 2)),
             dma((2,)),

time: 101 us -> 96.6 us (0.956)
  the two profiles are of different devices: /device:TPU:25 before, /device:TPU:1 now
where the time goes in v5:
time: 96.6 us; the launch traced here: 96.5 us
  Pallas kernels  95.7 us (99%)
    pallas_call x1, Pallas kernels, body(): pl.pallas_call(functools.partial(kernel, sections), out_shape=(jax.ShapeD...  91.1 us
    pallas_call x1, Pallas kernels, body(): pl.pallas_call(write_out, out_shape=(jax.ShapeDtypeStruct((rows, depth),...  4.66 us

profile of v5, /device:TPU:1, one launch (start us, length us, event | category | flops | bytes accessed | tf_op | source)
XLA Modules:
  0.0 96.5 jit_solution(2899462608539505041)
XLA Ops:
  0.6 91.1 %shard_map.101 = (bf16[256,4096]{1,0:T(8,128)(2,1)}, bf16[256,4096]{1,0:T(8,128)(2,1)}, bf16[512,512]{1,0:T(8,128)(2,1)}, bf16[512,512]{1,0:T(8,128)(2,1)}, bf16[512,512]{1,0:T(8,128)(2,1)}) custom-call(bf16[256,4096]{1,0:T(8,128)(2,1)} %tokens.1, f32[1,4096]{1,0:T(1,128)} %bitcast.1, bf16[4096,512]{1,0:T(8,128)(2,1)} %gate_hbm.1, bf16[4096,512]{1,0:T(8,128)(2,1)} %up_hbm.1, ...), custom_call_target="tpu_custom_call" | custom-call | flops 19327352832 | bytes 24117248 | tf_op jit(solution)/shard_map/pallas_call | solution.py:687
  91.7 4.7 %shard_map.102 = (bf16[256,4096]{1,0:T(8,128)(2,1)}, bf16[256,4096]{1,0:T(8,128)(2,1)}, f32[512,512]{1,0:T(8,128)}, f32[512,512]{1,0:T(8,128)}, f32[512,512]{1,0:T(8,128)}) custom-call(bf16[256,4096]{1,0:T(8,128)(2,1)} %get-tuple-element.10.layer_in, bf16[256,4096]{1,0:T(8,128)(2,1)} %get-tuple-element.11.input_in, ...), custom_call_target="tpu_custom_call" | custom-call | bytes 13631488 | tf_op jit(solution)/shard_map/pallas_call | solution.py:750

commit v6 on v5

--- a/solution.py
+++ b/solution.py
@@ -110,21 +110,18 @@
             device_id_type=MESH,
         )
 
-    loads = [
-        pltpu.make_async_copy(src, dst, load_sem.at[i])
-        for i, (src, dst) in enumerate(
-            (
-                (tokens, tok),
-                (gain_hbm, gain),
-                (gate_hbm, weight_in.at[GATE]),
-                (up_hbm, weight_in.at[UP]),
-                (cotangent, cot.at[pl.ds(0, rows)]),
-                (down_hbm, weight_down),
-            )
-        )
+    def load(i, src, dst):
+        return pltpu.make_async_copy(src, dst, load_sem.at[i])
+
+    load_rows = (load(0, tokens, tok), load(1, gain_hbm, gain))
+    load_in = [
+        load(2 + 2 * h + m, src.at[:, at], weight_in.at[m, :, at])
+        for h, at in enumerate((pl.ds(0, half), pl.ds(half, half)))
+        for m, src in enumerate((gate_hbm, up_hbm))
     ]
-    for load in loads:
-        load.start()
+    load_rest = (load(6, cotangent, cot.at[own]), load(7, down_hbm, weight_down))
+    for copy in (*load_rows, *load_in):
+        copy.start()
 
     barrier = pltpu.get_barrier_semaphore()
     for device in (to_before, to_after, partner, neighbour(0), neighbour(1)):
@@ -184,10 +181,21 @@
 
         lax.fori_loop(0, count // 16, step, 0, unroll=2)
 
-    def forward(first, count):
+    def forward(first, count, fresh=False, then=None):
         here = pl.ds(first, count)
 
         def step(h, _):
+            if fresh:
+                for m in range(2):
+
+                    @pl.when(h == 0)
+                    def _():
+                        load_in[m].wait()
+
+                    @pl.when(h == 1)
+                    def _():
+                        load_in[2 + m].wait()
+
             cols = pl.ds(pl.multiple_of(h * half, half), half)
             g = jnp.dot(normed[here], weight_in[GATE, :, cols], preferred_element_type=F32)
             u = jnp.dot(normed[here], weight_in[UP, :, cols], preferred_element_type=F32)
@@ -196,6 +204,8 @@
             hidden = g * jax.nn.sigmoid(g) * u
             acts[DOWN, here, cols] = hidden.astype(BF16)
             acts_t[DOWN, cols, here] = hidden.T.astype(BF16)
+            if then is not None:
+                then(h)
             return 0
 
         lax.fori_loop(0, 2, step, 0)
@@ -337,12 +347,12 @@
 
         return put
 
-    def down_tile(to_plane, to_x, put, adds):
+    def down_tile(to_plane, to_x, put, adds, part=whole):
         first = (to_plane * 2 + to_x) * piece
         for c in range(2):
             at = pl.ds(c * (piece // 2), piece // 2)
             cols = pl.ds(pl.multiple_of(first + c * (piece // 2), piece // 2), piece // 2)
-            acc = jnp.dot(acts_t[DOWN], cot[:, cols], preferred_element_type=F32)
+            acc = jnp.dot(acts_t[DOWN, part], cot[:, cols], preferred_element_type=F32)
             for ref in adds:
                 acc = acc + ref[:, at].astype(F32)
             put(at, acc)
@@ -359,8 +369,9 @@
 
         lax.fori_loop(0, 2, run, 0)
 
-    def copy_a1(way):
-        return remote(a1_out.at[way], a1_in.at[way], a1_sem.at[way], neighbour(way))
+    def copy_a1(way, h):
+        at = half_rows(h)
+        return remote(a1_out.at[way, at], a1_in.at[way, at], a1_sem.at[way, h], neighbour(way))
 
     def copy_a2(way, merged):
         src = a1_in.at[way] if merged else a2_out.at[way]
@@ -368,16 +379,22 @@
 
     copy_ax = remote(a2_in.at[0, xl], ax_in, ax_sem, partner)
 
-    def a_opposite(way):
-        down_tile(plane(2), way, into(a1_out.at[way]), ())
-        copy_a1(way).start()
+    def a_opposite(h):
+        at = half_rows(h)
+
+        def send(way):
+            down_tile(plane(2), way, into(a1_out.at[way, at]), (), at)
+            copy_a1(way, h).start()
+
+        two(send)
 
     def a_direct(way):
         down_tile(plane(1 + 2 * way), 1 - way, into(a2_out.at[way]), ())
         copy_a2(way, 0).start()
 
     def a_merged(way):
-        copy_a1(way).wait_recv()
+        copy_a1(way, 0).wait_recv()
+        copy_a1(way, 1).wait_recv()
         here = a1_in.at[way]
         down_tile(plane(1 + 2 * way), way, into(here), (here,))
         copy_a2(way, 1).start()
@@ -492,26 +509,26 @@
             result[m, at] = (total * factor).astype(BF16)
         return store(m, out)
 
-    loads[0].wait()
-    loads[1].wait()
+    for copy in load_rows:
+        copy.wait()
+    for copy in load_rest:
+        copy.start()
     normalize(tok, 0, rows, True)
     start_near(0)
     start_near(1)
 
     @pl.when(core == 0)
     def _():
-        loads[2].wait()
-        loads[3].wait()
-        forward(0, rows)
+        forward(0, rows, True)
         for copy in send_tok:
             copy.wait_recv()
         normalize(normed, rows, rows, False)
-        forward(rows, rows)
-        loads[4].wait()
-        loads[5].wait()
-        for copy in send_cot:
+        for copy in load_rest:
+            copy.wait()
+        send_cot[0].wait_recv()
+        forward(rows, rows, then=a_opposite)
+        for copy in send_cot[1:]:
             copy.wait_recv()
-        two(a_opposite)
         backward(0, 2 * rows)
         copy_far(GATE).start()
         two(a_direct)
@@ -526,11 +543,9 @@
 
     @pl.when(core == 1)
     def _():
-        loads[2].wait()
-        loads[3].wait()
-        forward(0, rows)
-        loads[4].wait()
-        loads[5].wait()
+        forward(0, rows, True)
+        for copy in load_rest:
+            copy.wait()
         backward(0, rows)
         own_grad()
         pass_on(0)
@@ -607,7 +622,8 @@
             copy_pass(zz).wait_send()
 
     for i in range(2):
-        copy_a1(i).wait_send()
+        copy_a1(i, 0).wait_send()
+        copy_a1(i, 1).wait_send()
         copy_far(i).wait_send()
         for k in range(2):
             copy_a2(i, k).wait_send()
@@ -632,44 +648,41 @@
     far,
     sems,
 ):
-    loads = [
-        pltpu.make_async_copy(src, dst, sems.at[0, i])
-        for i, (src, dst) in enumerate(
-            (
-                (gate_in, near.at[GATE]),
-                (up_in, near.at[UP]),
-                (down_in, near.at[DOWN]),
-                (layer_in, rows.at[0]),
-                (input_in, rows.at[1]),
+    pieces = 4
+    count = layer_in.shape[0] // pieces
+    moves = []
+    for k, (src, dst) in enumerate(((layer_in, layer_out), (input_in, input_grad))):
+        for i in range(pieces):
+            at, sem = pl.ds(i * count, count), 3 + k * pieces + i
+            moves.append(
+                (
+                    pltpu.make_async_copy(src.at[at], rows.at[k, at], sems.at[0, sem]),
+                    pltpu.make_async_copy(rows.at[k, at], dst.at[at], sems.at[1, sem]),
+                )
             )
+    grads = [
+        (
+            pltpu.make_async_copy(src, near.at[m], sems.at[0, m]),
+            pltpu.make_async_copy(far.at[m], dst, sems.at[1, m]),
+        )
+        for m, (src, dst) in enumerate(
+            ((gate_in, gate_grad), (up_in, up_grad), (down_in, down_grad))
         )
     ]
-    stores = [
-        pltpu.make_async_copy(src, dst, sems.at[1, i])
-        for i, (src, dst) in enumerate(
-            (
-                (far.at[GATE], gate_grad),
-                (far.at[UP], up_grad),
-                (far.at[DOWN], down_grad),
-                (rows.at[0], layer_out),
-                (rows.at[1], input_grad),
-            )
-        )
-    ]
-    for i in (3, 4, 0, 1, 2):
-        loads[i].start()
-    for i in (3, 4):
-        loads[i].wait()
-        stores[i].start()
-    for m in (GATE, UP, DOWN):
-        loads[m].wait()
+    for load, _ in grads + moves:
+        load.start()
+    for m, (load, store) in enumerate(grads):
+        load.wait()
         if m == DOWN:
             far[m] = near[m].astype(F32)
         else:
             far[m] = near[m].astype(F32).T
-        stores[m].start()
-    for copy in stores:
-        copy.wait()
+        store.start()
+    for load, store in moves:
+        load.wait()
+        store.start()
+    for _, store in grads + moves:
+        store.wait()
 
 
 def body(sections, tokens, norm_gain, gate_weight, up_weight, down_weight, cotangent):
@@ -726,11 +739,11 @@
             vmem(2, 2, half, piece),
             vmem(2, 2, 2, half, piece),
             vmem(3, ff, piece),
-            dma((6,)),
+            dma((8,)),
             dma((5,)),
             dma((6, 2)),
             dma((6, 2)),
-            dma((2, 2)),
+            dma((2, 2, 2)),
             dma((2, 2, 2)),
             dma((2,)),
             dma((4, 2)),
@@ -762,7 +775,7 @@
             vmem(2, rows, depth),
             vmem(3, ff, piece),
             vmem(3, ff, piece, dtype=F32),
-            dma((2, 5)),
+            dma((2, 11)),
         ],
         compiler_params=pltpu.CompilerParams(vmem_limit_bytes=63 * 2**20),
         cost_estimate=pl.CostEstimate(flops=0, bytes_accessed=13 * 2**20, transcendentals=0),

time: 96.6 us -> 95.2 us (0.986)
  Pallas kernels: 95.7 us -> 94.3 us
    pallas_call x1, Pallas kernels: 91.1 us -> 89.6 us  [body(): pl.pallas_call(functools.partial(kernel, sections), out_shape=(jax.ShapeD...]
where the time goes in v6:
time: 95.2 us; the launch traced here: 95.1 us
  Pallas kernels  94.3 us (99%)
    pallas_call x1, Pallas kernels, body(): pl.pallas_call(functools.partial(kernel, sections), out_shape=(jax.ShapeD...  89.6 us
    pallas_call x1, Pallas kernels, body(): pl.pallas_call(write_out, out_shape=(jax.ShapeDtypeStruct((rows, depth),...  4.72 us

profile of v6, /device:TPU:1, one launch (start us, length us, event | category | flops | bytes accessed | tf_op | source)
XLA Modules:
  0.0 95.1 jit_solution(5410462812027718107)
XLA Ops:
  0.6 89.6 %shard_map.101 = (bf16[256,4096]{1,0:T(8,128)(2,1)}, bf16[256,4096]{1,0:T(8,128)(2,1)}, bf16[512,512]{1,0:T(8,128)(2,1)}, bf16[512,512]{1,0:T(8,128)(2,1)}, bf16[512,512]{1,0:T(8,128)(2,1)}) custom-call(bf16[256,4096]{1,0:T(8,128)(2,1)} %tokens.1, f32[1,4096]{1,0:T(1,128)} %bitcast.1, bf16[4096,512]{1,0:T(8,128)(2,1)} %gate_hbm.1, bf16[4096,512]{1,0:T(8,128)(2,1)} %up_hbm.1, ...), custom_call_target="tpu_custom_call" | custom-call | flops 19327352832 | bytes 24117248 | tf_op jit(solution)/shard_map/pallas_call | solution.py:700
  90.3 4.7 %shard_map.102 = (bf16[256,4096]{1,0:T(8,128)(2,1)}, bf16[256,4096]{1,0:T(8,128)(2,1)}, f32[512,512]{1,0:T(8,128)}, f32[512,512]{1,0:T(8,128)}, f32[512,512]{1,0:T(8,128)}) custom-call(bf16[256,4096]{1,0:T(8,128)(2,1)} %get-tuple-element.10.layer_in, bf16[256,4096]{1,0:T(8,128)(2,1)} %get-tuple-element.11.input_in, ...), custom_call_target="tpu_custom_call" | custom-call | bytes 13631488 | tf_op jit(solution)/shard_map/pallas_call | solution.py:763

commit v7 on v6

--- a/solution.py
+++ b/solution.py
@@ -179,7 +179,7 @@
             normed[to] = (values * inv * gain[...]).astype(BF16)
             return 0
 
-        lax.fori_loop(0, count // 16, step, 0, unroll=2)
+        lax.fori_loop(0, count // 16, step, 0, unroll=4)
 
     def forward(first, count, fresh=False, then=None):
         here = pl.ds(first, count)
@@ -676,7 +676,7 @@
         if m == DOWN:
             far[m] = near[m].astype(F32)
         else:
-            far[m] = near[m].astype(F32).T
+            far[m] = near[m].T.astype(F32)
         store.start()
     for load, store in moves:
         load.wait()

time: 95.2 us -> 94.9 us (level)
  no operation moved by 1% of the time
where the time goes in v7:
time: 94.9 us; the launch traced here: 94.8 us
  Pallas kernels  94 us (99%)
    pallas_call x1, Pallas kernels, body(): pl.pallas_call(functools.partial(kernel, sections), out_shape=(jax.ShapeD...  89.2 us
    pallas_call x1, Pallas kernels, body(): pl.pallas_call(write_out, out_shape=(jax.ShapeDtypeStruct((rows, depth),...  4.74 us

profile of v7, /device:TPU:1, one launch (start us, length us, event | category | flops | bytes accessed | tf_op | source)
XLA Modules:
  0.0 94.8 jit_solution(6996040455589753017)
XLA Ops:
  0.6 89.2 %shard_map.101 = (bf16[256,4096]{1,0:T(8,128)(2,1)}, bf16[256,4096]{1,0:T(8,128)(2,1)}, bf16[512,512]{1,0:T(8,128)(2,1)}, bf16[512,512]{1,0:T(8,128)(2,1)}, bf16[512,512]{1,0:T(8,128)(2,1)}) custom-call(bf16[256,4096]{1,0:T(8,128)(2,1)} %tokens.1, f32[1,4096]{1,0:T(1,128)} %bitcast.1, bf16[4096,512]{1,0:T(8,128)(2,1)} %gate_hbm.1, bf16[4096,512]{1,0:T(8,128)(2,1)} %up_hbm.1, ...), custom_call_target="tpu_custom_call" | custom-call | flops 19327352832 | bytes 24117248 | tf_op jit(solution)/shard_map/pallas_call | solution.py:700
  89.9 4.7 %shard_map.102 = (bf16[256,4096]{1,0:T(8,128)(2,1)}, bf16[256,4096]{1,0:T(8,128)(2,1)}, f32[512,512]{1,0:T(8,128)}, f32[512,512]{1,0:T(8,128)}, f32[512,512]{1,0:T(8,128)}) custom-call(bf16[256,4096]{1,0:T(8,128)(2,1)} %get-tuple-element.10.layer_in, bf16[256,4096]{1,0:T(8,128)(2,1)} %get-tuple-element.11.input_in, ...), custom_call_target="tpu_custom_call" | custom-call | bytes 13631488 | tf_op jit(solution)/shard_map/pallas_call | solution.py:763
